TPU v7x, 512 devices: a whole 4x4x16 slice. The times are simulated.
512 devices in a mesh: res: 128 (over y, x, z_lo), depth: 4 (over z_hi, core).
Axes of the slice: x: 4, y: 4, z: 16 (z_hi: 2, z_lo: 8; z = z_hi * 8 + z_lo), core: 2. Of those that a mesh axis runs over, the one named last changes fastest.
Arguments:
- alignment_embedding: bfloat16 [512, 512, 256], P('depth', 'res'), may hold values from -6 to 6
- standardizer_gain: float32 [256], replicated, may hold values from 0.1 to 1.9
- standardizer_offset: float32 [256], replicated, may hold values from -3 to 3
- first_factor_matrix: bfloat16 [256, 32], replicated, may hold values from -0.375 to 0.375
- first_factor_offset: float32 [32], replicated, may hold values from -0.6 to 0.6
- second_factor_matrix: bfloat16 [256, 32], replicated, may hold values from -0.375 to 0.375
- second_factor_offset: float32 [32], replicated, may hold values from -0.6 to 0.6
- final_mapping_matrix: bfloat16 [1024, 128], replicated, may hold values from -4 to 4
- final_offset_entries: float32 [128], replicated, may hold values from -3 to 3
Outputs:
- pair: bfloat16 [512, 512, 128], P(('res', 'depth'))
All inputs are finite; a program needn't handle non-finite values.
Results may differ from a plain program's by a relative error of at most 0.015.
Values may be sent and summed in bfloat16 or wider, within the bound.
No kernel may reach another device: no remote copies, remote signals or barrier semaphores. Data moves between devices by JAX's collectives and lax.ppermute only.
A program may use at most 64 MiB of HBM per device.

v0:
```python
import math

import jax
import jax.numpy as jnp
from jax import lax
from jax.sharding import PartitionSpec as P


def standardize_features(alignment_embedding, standardizer_gain, standardizer_offset):
    entry_tensor = alignment_embedding.astype(jnp.float32)
    centre = jnp.mean(entry_tensor, axis=-1, keepdims=True)
    spread = jnp.mean((entry_tensor - centre) ** 2, axis=-1, keepdims=True)
    return (
        (entry_tensor - centre) * lax.rsqrt(spread + 1e-05) * standardizer_gain
        + standardizer_offset
    ).astype(jnp.bfloat16)


def contract(left_grp, piece, w_three, inverse):
    groups, chain_rows, left_cols = left_grp.shape
    chans = w_three.shape[0]
    rows_left = left_cols // chans
    count = piece.shape[2]
    flat_piece = piece.reshape(groups, chain_rows, count * chans)
    extent = math.gcd(count, 32)

    def one(index):
        part = lax.dynamic_slice_in_dim(flat_piece, index * extent * chans, extent * chans, 2)
        outer = lax.dot_general(
            left_grp, part, (((1,), (1,)), ((0,), (0,))), preferred_element_type=jnp.float32
        )
        outer = (
            (outer * inverse).astype(jnp.bfloat16).reshape(groups, rows_left, chans, extent, chans)
        )
        return jnp.einsum("gicje,cez->ijz", outer, w_three, preferred_element_type=jnp.float32)

    result = lax.map(one, jnp.arange(count // extent, dtype=jnp.int32))
    result = jnp.moveaxis(result, 0, 1)
    return result.reshape(rows_left, count, w_three.shape[2])


def local(
    alignment_embedding,
    standardizer_gain,
    standardizer_offset,
    first_factor_matrix,
    first_factor_offset,
    second_factor_matrix,
    second_factor_offset,
    final_mapping_matrix,
    final_offset_entries,
):
    chain_rows, residue_rows, feature_width = alignment_embedding.shape
    chans = first_factor_matrix.shape[1]
    groups = lax.axis_size("depth")
    inverse = 1.0 / (chain_rows * groups)
    w_three = final_mapping_matrix.reshape(chans, chans, final_mapping_matrix.shape[1])
    standardized_alignment = standardize_features(
        alignment_embedding, standardizer_gain, standardizer_offset
    ).reshape(chain_rows * residue_rows, feature_width)
    left = (
        jnp.dot(standardized_alignment, first_factor_matrix, preferred_element_type=jnp.float32)
        + first_factor_offset
    ).astype(jnp.bfloat16)
    right = (
        jnp.dot(standardized_alignment, second_factor_matrix, preferred_element_type=jnp.float32)
        + second_factor_offset
    ).astype(jnp.bfloat16)
    left_grp = left.reshape(1, chain_rows, residue_rows * chans)
    right_three = right.reshape(chain_rows, residue_rows, chans)
    piece = lax.all_gather(right_three, "res", axis=1, tiled=True)
    terms = contract(
        left_grp, piece.reshape(1, chain_rows, piece.shape[1], chans), w_three, inverse
    )
    summed = lax.psum_scatter(
        terms.astype(jnp.bfloat16), "depth", scatter_dimension=0, tiled=True
    ).astype(jnp.float32)
    return (summed + final_offset_entries).astype(jnp.bfloat16)


def solution(mesh):
    placed = (P("depth", "res", None), P(), P(), P(), P(), P(), P(), P(), P())
    return jax.shard_map(
        local,
        mesh=mesh,
        in_specs=placed,
        out_specs=P(("res", "depth"), None, None),
        check_vma=False,
    )
```

profile of v0, /device:TPU:1, one launch (start us, length us, event | category | flops | bytes accessed | tf_op | source)
XLA Modules:
  0.0 1134.1 jit_solution(12624233033913176081)
XLA Ops:
  6.5 1.2 convert_reduce_fusion
  7.7 1.3 fusion.12
  9.1 1.3 fusion.15
  10.5 0.8 fusion.8
  11.5 0.7 copy.21
  12.3 0.9 fusion.9
  13.4 887.9 %all-gather.2.cloned.1.call-done = bf16[128,512,32]{0,2,1:T(8,128)(2,1)} async-done(((bf16[128,4,32]{0,2,1:T(8,128)(2,1)}), bf16[128,512,32]{0,2,1:T(8,128)(2,1)}) %all-gather.2.cloned.1.call-update) | async-done | bytes 4194320 | tf_op jit(solution)/shard_map/all_gather | solution.py:71
  901.3 85.3 %while.12 = (s32[]{:T(128)}, bf16[16,4,32,128]{3,2,1,0:T(8,128)(2,1)S(1)}, s32[16]{0:T(128)S(1)}, bf16[1,128,16384]{1,2,0:T(8,128)(2,1)}, bf16[1,128,128]{2,1,0:...) while((s32[]{:T(128)}, ...), condition=%wide.region_3.0_spmd, body=%wide.region_2.3_spmd.sunk | while | flops 67371008 | bytes 2982055 | solution.py:37
  902.6 1.2 fusion.31
  904.2 1.1 copy.28
  905.3 1.3 fusion.32
  906.7 0.6 dynamic_slice.20
  907.9 1.2 fusion.31
  909.5 1.1 copy.28
  910.6 1.3 fusion.32
  912.0 0.6 dynamic_slice.20
  913.2 1.2 fusion.31
  914.8 1.1 copy.28
  916.0 1.3 fusion.32
  918.6 1.2 fusion.31
  920.2 1.1 copy.28
  921.3 1.3 fusion.32
  922.7 0.6 dynamic_slice.20
  923.9 1.2 fusion.31
  925.5 1.1 copy.28
  926.6 1.3 fusion.32
  928.0 0.6 dynamic_slice.20
  929.2 1.2 fusion.31
  930.8 1.1 copy.28
  932.0 1.3 fusion.32
  934.6 1.2 fusion.31
  936.2 1.1 copy.28
  937.3 1.3 fusion.32
  938.7 0.6 dynamic_slice.20
  939.9 1.2 fusion.31
  941.5 1.1 copy.28
  942.7 1.3 fusion.32
  945.3 1.2 fusion.31
  946.8 1.1 copy.28
  948.0 1.3 fusion.32
  950.6 1.2 fusion.31
  952.2 1.1 copy.28
  953.3 1.3 fusion.32
  955.9 1.2 fusion.31
  957.5 1.1 copy.28
  958.7 1.3 fusion.32
  961.3 1.2 fusion.31
  962.9 1.1 copy.28
  964.0 1.3 fusion.32
  966.6 1.2 fusion.31
  968.2 1.1 copy.28
  969.3 1.3 fusion.32
  971.9 1.2 fusion.31
  973.5 1.1 copy.28
  974.7 1.3 fusion.32
  977.3 1.2 fusion.31
  978.9 1.1 copy.28
  980.0 1.3 fusion.32
  982.6 1.2 fusion.31
  984.2 1.1 copy.28
  985.3 1.3 fusion.32
  986.7 0.8 copy.24
  987.6 138.1 %reduce-scatter.2.cloned.1.call-done = bf16[1,512,128]{2,1,0:T(8,128)(2,1)} async-done(((bf16[4,512,128]{2,1,0:T(8,128)(2,1)}), bf16[1,512,128]{2,1,0:T(8,128)(2,1)}) %reduce-scatter.2.cloned.1.call-update) | async-done | bytes 131088 | tf_op jit(solution)/shard_map/reduce_scatter | solution.py:75
  1125.7 1.6 add_convert_fusion
  (43 shorter events, 13.5 us)
Async XLA Ops:
  6.5 3.9 copy-start
  6.5 894.8 %all-gather.2.cloned.1.call-start = ((), (), s32[]{:S(2)}) async-start(), calls=%async_computation.1 | async-start | bytes 4227072 | tf_op jit(solution)/shard_map/all_gather | solution.py:71
  12.2 1113.5 %reduce-scatter.2.cloned.1.call-start = ((), (), s32[]{:S(2)}) async-start(), calls=%async_computation.2 | async-start | bytes 655360 | tf_op jit(solution)/shard_map/reduce_scatter | solution.py:75
  901.3 224.4 %copy-start.1 = (f32[128]{0:T(128)S(1)}, f32[128]{0:T(128)}, u32[]{:S(2)}) copy-start(f32[128]{0:T(128)} %param.19) | copy-start | bytes 1540
Sparse Core Ops, SparseCore 0:
  12.3 888.9 all-gather.1
  987.7 137.9 reduce-scatter.1
where the time goes:
time: 1140 us; the launch traced here: 1130 us
  waiting for transfers between devices  1030 us (90%)
  matrix products  41.7 us (4%)
  local copies, waits for them, and re-layouts  36.2 us (3%)
  between operations  13.5 us (1%)
    all_gather x1, waiting for transfers between devices, local(): piece = lax.all_gather(right_three, 'res', axis=1, tiled=True)  888 us
    reduce_scatter x1, waiting for transfers between devices, local(): lax.psum_scatter(terms.astype(jnp.bfloat16), 'depth', scatter_dimension=0...  138 us
    reduce_sum x32, local copies, waits for them, and re-layouts, one(): jnp.einsum('gicje,cez->ijz', outer, w_three, preferred_element_type=jnp.f...  24.8 us
  transfers between devices with their start and end apart: 2, of which 2 were waited for; matrix products, arithmetic and copies ran while one was open for 0% of the time, Pallas kernels for 0%

commit v1 on v0

v1 whole, which is shorter than its diff:
```python
import jax
import jax.numpy as jnp
from jax import lax
from jax.experimental import pallas as pl
from jax.experimental.pallas import tpu as pltpu
from jax.sharding import Mesh, PartitionSpec as P

F32 = jnp.float32
BF16 = jnp.bfloat16
AXES = ("y", "x", "zq", "zp", "zh", "core")
SWAP = [(0, 1), (1, 0)]
NT = (((1,), (1,)), ((), ()))


def project(x_ref, gain_ref, offset_ref, matrix_ref, bias_ref):
    x = x_ref[...].astype(F32)
    centre = jnp.mean(x, axis=-1, keepdims=True)
    shifted = x - centre
    spread = jnp.mean(shifted * shifted, axis=-1, keepdims=True)
    normed = shifted * lax.rsqrt(spread + 1e-05) * gain_ref[...].reshape(1, 1, -1)
    normed = normed + offset_ref[...].reshape(1, 1, -1)
    chain_rows, residue_rows, _ = x.shape
    chans = matrix_ref.shape[1]
    matrix = matrix_ref[...].astype(F32).T.astype(BF16)
    bias = jnp.broadcast_to(bias_ref[...], (chain_rows, chans)).T
    return [
        lax.dot_general(matrix, normed[:, r, :].astype(BF16), NT, preferred_element_type=F32) + bias
        for r in range(residue_rows)
    ]


def right_kernel(x_ref, gain_ref, offset_ref, matrix_ref, bias_ref, out_ref):
    parts = project(x_ref, gain_ref, offset_ref, matrix_ref, bias_ref)
    out_ref[...] = jnp.concatenate(parts, axis=0).astype(BF16)


def left_kernel(x_ref, gain_ref, offset_ref, matrix_ref, bias_ref, own_ref, other_ref):
    parts = project(x_ref, gain_ref, offset_ref, matrix_ref, bias_ref)
    first = jnp.concatenate(parts[:2], axis=0)
    second = jnp.concatenate(parts[2:], axis=0)
    low = lax.axis_index("zh") == 0
    own_ref[...] = jnp.where(low, first, second).astype(BF16)
    other_ref[...] = jnp.where(low, second, first).astype(BF16)


def pair_kernel(own_ref, near_ref, left_ref, map_ref, out_ref, a32, a16, x16, wide, res):
    zh = lax.axis_index("zh")
    zp = lax.axis_index("zp")
    for yx in range(16):
        for block in range(2):
            for ii in range(2):
                a32[pl.ds(block * 1024 + yx * 2 + ii, 32, stride=32), :] = left_ref[
                    yx, block, ii * 32 : ii * 32 + 32, :
                ].astype(F32)
    for block in range(2):
        a16[:, block * 128 : block * 128 + 128] = a32[block * 1024 : block * 1024 + 1024, :].astype(BF16)
    wide[...] = jnp.zeros_like(wide)
    for c in range(32):
        for r in range(4):
            wide[c * 128 + r * 32 : c * 128 + r * 32 + 32, r * 128 : r * 128 + 128] = map_ref[
                c * 32 : c * 32 + 32, :
            ]
    for zl in range(8):
        zq, parity = zl // 2, zl % 2
        mine = zp == parity
        blocks = []
        for src in (zh, 1 - zh):
            blocks.append(jnp.where(mine, own_ref[src * 4 + zq], near_ref[src * 4 + zq]))
        right = jnp.concatenate(blocks, axis=1)
        outer = lax.dot_general(a16[...], right, NT, preferred_element_type=F32).astype(BF16)
        for c in range(32):
            x16[zl * 32 : zl * 32 + 32, c * 128 : c * 128 + 128] = outer[c * 32 : c * 32 + 32, :]
    total = jnp.dot(x16[...], wide[...], preferred_element_type=F32) * (1.0 / 512)
    for r in range(4):
        res[r * 256 : r * 256 + 256, :] = total[:, r * 128 : r * 128 + 128]
    for r in range(4):
        for i in range(0, 32, 2):
            rows = [res[pl.ds(r * 256 + i + k, 8, stride=32), :] for k in range(2)]
            out_ref[i * 8 : i * 8 + 16, r * 128 : r * 128 + 128] = jnp.concatenate(rows, axis=0).astype(BF16)


def final_kernel(parts_ref, bias_ref, out_ref, rows):
    parts = parts_ref[...].astype(F32).reshape(16, 2, 8, 512)
    summed = (parts[:, 0] + parts[:, 1]).reshape(128, 512)
    for r in range(4):
        rows[pl.ds(r, 128, stride=4), :] = summed[:, r * 128 : r * 128 + 128] + bias_ref[...]
    out_ref[...] = rows[...].astype(BF16)


def params(mib):
    return pltpu.CompilerParams(vmem_limit_bytes=mib * 2**20)


def local(x, gain, offset, first, first_bias, second, second_bias, mapping, final_bias):
    gain, offset = gain.reshape(1, -1), offset.reshape(1, -1)
    right = pl.pallas_call(
        right_kernel,
        out_shape=jax.ShapeDtypeStruct((128, 128), BF16),
        compiler_params=params(16),
        name="right_projection",
    )(x, gain, offset, second, second_bias.reshape(1, -1))
    half = jax.ShapeDtypeStruct((64, 128), BF16)
    left_own, left_other = pl.pallas_call(
        left_kernel,
        out_shape=(half, half),
        compiler_params=params(16),
        name="left_projection",
    )(x, gain, offset, first, first_bias.reshape(1, -1))

    own = lax.all_to_all(jnp.broadcast_to(right[None], (8, 128, 128)), ("zh", "zq"), 0, 0)
    left_got = lax.ppermute(left_other, "zh", SWAP)
    left = jnp.stack([left_own, left_got])
    left, own = lax.optimization_barrier((left, own))
    near = lax.ppermute(own, "zp", SWAP)
    left = lax.all_to_all(jnp.broadcast_to(left[None], (16, 2, 64, 128)), ("y", "x"), 0, 0)

    parts = pl.pallas_call(
        pair_kernel,
        out_shape=jax.ShapeDtypeStruct((256, 512), BF16),
        scratch_shapes=[
            pltpu.VMEM((2048, 128), F32),
            pltpu.VMEM((1024, 256), BF16),
            pltpu.VMEM((256, 4096), BF16),
            pltpu.VMEM((4096, 512), BF16),
            pltpu.VMEM((1024, 128), F32),
        ],
        compiler_params=params(40),
        name="pair_block",
    )(own, near, left, mapping)
    parts = lax.all_to_all(parts.reshape(32, 8, 512), ("y", "x", "core"), 0, 0)
    out = pl.pallas_call(
        final_kernel,
        out_shape=jax.ShapeDtypeStruct((512, 128), BF16),
        scratch_shapes=[pltpu.VMEM((512, 128), F32)],
        compiler_params=params(16),
        name="sum_and_bias",
    )(parts.reshape(256, 512), final_bias.reshape(1, -1))
    return out.reshape(1, 512, 128)


def solution(mesh):
    fine = Mesh(mesh.devices.reshape(4, 4, 4, 2, 2, 2), AXES)
    placed = (P(("zh", "core"), ("y", "x", "zq", "zp"), None),) + (P(),) * 8
    return jax.shard_map(
        local, mesh=fine, in_specs=placed, out_specs=P(AXES, None, None), check_vma=False
    )
```

time: 1140 us -> 82 us (0.07)
  waiting for transfers between devices: 1030 us -> 10.9 us
  matrix products: 41.7 us -> 0 us
  starting transfers between devices: 0.04 us -> 36.7 us
  local copies, waits for them, and re-layouts: 36.2 us -> 5.53 us
  blocking collectives: 0 us -> 21.6 us
  between operations: 13.5 us -> 0.1 us
    all_gather x1 -> x0, waiting for transfers between devices: 888 us -> none  [local(): piece = lax.all_gather(right_three, 'res', axis=1, tiled=True)]
    reduce_scatter x1 -> x0, waiting for transfers between devices: 138 us -> none  [local(): lax.psum_scatter(terms.astype(jnp.bfloat16), 'depth', scatter_dimension=0...]
    dot_general x34 -> x0, matrix products: 41.7 us -> none  [the longest x16 21.3 us: one(): jnp.einsum('gicje,cez->ijz', outer, w_three, preferred_element_type=jnp.f...]
    reduce_sum x32 -> x0, local copies, waits for them, and re-layouts: 24.8 us -> none  [one(): jnp.einsum('gicje,cez->ijz', outer, w_three, preferred_element_type=jnp.f...]
    all_to_all x0 -> x2, starting transfers between devices: none -> 22.7 us  [the longest x1 15.8 us: local(): lax.all_to_all(jnp.broadcast_to(right[None], (8, 128, 128)), ('zh', 'zq')...]
    all_to_all x0 -> x1, blocking collectives: none -> 21.6 us  [local(): parts = lax.all_to_all(parts.reshape(32, 8, 512), ('y', 'x', 'core'), 0, 0)]
    ppermute x0 -> x2, starting transfers between devices: none -> 14.1 us  [the longest x1 12.1 us: local(): left_got = lax.ppermute(left_other, 'zh', SWAP)]
  transfers between devices with their start and end apart: 2 -> 4, of which waited for: 2 -> 3; matrix products, arithmetic and copies ran while one was open for 0% -> 0% of each run, Pallas kernels for 0% -> 1%
where the time goes in v1:
time: 82 us; the launch traced here: 81.5 us
  starting transfers between devices  36.7 us (45%)
  blocking collectives  21.6 us (26%)
  waiting for transfers between devices  10.9 us (13%)
  Pallas kernels  6.57 us (8%)
  local copies, waits for them, and re-layouts  5.53 us (7%)
    all_to_all x1, blocking collectives, local(): parts = lax.all_to_all(parts.reshape(32, 8, 512), ('y', 'x', 'core'), 0, 0)  21.6 us
    all_to_all x1, starting transfers between devices, local(): lax.all_to_all(jnp.broadcast_to(right[None], (8, 128, 128)), ('zh', 'zq')...  15.8 us
    ppermute x1, starting transfers between devices, local(): left_got = lax.ppermute(left_other, 'zh', SWAP)  12.1 us
    all_to_all x1, starting transfers between devices, local(): lax.all_to_all(jnp.broadcast_to(left[None], (16, 2, 64, 128)), ('y', 'x')...  6.89 us
    ppermute x1, waiting for transfers between devices, local(): near = lax.ppermute(own, 'zp', SWAP)  5.1 us
    ppermute x1, waiting for transfers between devices, local(): left_got = lax.ppermute(left_other, 'zh', SWAP)  3.96 us
    unnamed x20, local copies, waits for them, and re-layouts  3.89 us
    pallas_call x1, Pallas kernels, local(): pl.pallas_call(pair_kernel, out_shape=jax.ShapeDtypeStruct((256, 512), BF...  3.59 us
  transfers between devices with their start and end apart: 4, of which 3 were waited for; matrix products, arithmetic and copies ran while one was open for 0% of the time, Pallas kernels for 1%

profile of v1, /device:TPU:1, one launch (start us, length us, event | category | flops | bytes accessed | tf_op | source)
XLA Modules:
  0.0 81.5 jit_solution(17819002281249691426)
XLA Ops:
  0.0 0.8 %copy.11.matrix_ref = bf16[256,32]{1,0:T(8,128)(2,1)S(1)} copy(bf16[256,32]{0,1:T(8,128)(2,1)} %param.14) | data formatting | bytes 32768 | tf_op args[5]
  0.8 0.0 copy-start.4
  0.8 0.0 copy-start.3
  0.9 0.0 copy-start.5
  0.9 0.6 copy-done.4
  1.5 0.0 copy-done.3
  1.5 0.0 copy-done.5
  1.5 0.0 copy-start
  1.5 0.9 %copy-done = bf16[128,4,256]{2,1,0:T(4,128)(2,1)S(1)} copy-done((bf16[128,4,256]{2,1,0:T(4,128)(2,1)S(1)}, bf16[128,4,256]{2,1,0:T(4,128)(2,1)}, u32[]{:S(2)}) %copy-start) | copy-done | bytes 262168
  2.5 1.1 %right_projection.1 = bf16[128,128]{1,0:T(8,128)(2,1)S(1)} custom-call(bf16[128,4,256]{2,1,0:T(4,128)(2,1)S(1)} %copy-done, f32[1,256]{1,0:T(1,128)S(1)} %bitcast.13, f32[1,256]{1,0:T(1,128)S(1)} %bitcast.15, bf16[256,32]{1,0:T(8,128)(2,1)S(1)} %copy.11.matrix_ref, f32[1,32]{1,0:T(1,128)S(1)} %bitcast.17), custom_call_target="tpu_custom_call" | custom-call | tf_op jit(solution)/shard_map/right_projection/pallas_call | solution.py:96
  3.6 0.7 broadcast_in_dim.4
  4.4 0.0 copy-start.8
  4.4 0.0 copy-start.1
  4.4 15.8 %all-to-all-start = ((bf16[8,128,128]{2,1,0:T(8,128)(2,1)}), bf16[8,128,128]{2,1,0:T(8,128)(2,1)S(1)}, u32[]{:S(2)}, u32[]{:S(2)}) async-start(bf16[8,128,128]{2,1,0:T(8,128)(2,1)} %broadcast_in_dim.4), calls=%async_computation | async-start | bytes 524288 | tf_op jit(solution)/shard_map/all_to_all | solution.py:110
  20.1 0.0 copy-done.8
  20.1 0.1 copy.10.matrix_ref
  20.3 0.0 copy-start.6
  20.3 0.0 copy-done.1
  20.3 0.6 copy-done.6
  20.9 1.1 %left_projection.1 = (bf16[64,128]{1,0:T(8,128)(2,1)S(1)}, bf16[64,128]{1,0:T(8,128)(2,1)S(1)}) custom-call(bf16[128,4,256]{2,1,0:T(4,128)(2,1)S(1)} %copy-done.1, f32[1,256]{1,0:T(1,128)S(1)} %bitcast.14, f32[1,256]{1,0:T(1,128)S(1)} %bitcast.16, bf16[256,32]{1,0:T(8,128)(2,1)S(1)} %copy.10.matrix_ref, f32[1,32]{1,0:T(1,128)S(1)} %bitcast.18), custom_call_target="tpu_custom_call" | custom-call | tf_op jit(solution)/shard_map/left_projection/pallas_call | solution.py:103
  22.0 12.1 %collective-permute-start = (bf16[64,128]{1,0:T(8,128)(2,1)S(1)}, bf16[64,128]{1,0:T(8,128)(2,1)S(1)}, u32[]{:S(2)}, u32[]{:S(2)}) collective-permute-start(bf16[64,128]{1,0:T(8,128)(2,1)S(1)} %get-tuple-element.10), channel_id=1, source_target_pairs={{0,2},{2,0},{1,3},{3,1},{4,6},{6,4},{5,7},{7,5},{8,10},{10,8},{9,1... | collective-permute-start | bytes 49160 | tf_op jit(solution)/shard_map/ppermute | solution.py:111
  34.1 4.0 %collective-permute-done = bf16[64,128]{1,0:T(8,128)(2,1)S(1)} collective-permute-done((bf16[64,128]{1,0:T(8,128)(2,1)S(1)}, bf16[64,128]{1,0:T(8,128)(2,1)S(1)}, u32[]{:S(2)}, u32[]{:S(2)}) %collective-permute-start) | collective-permute-done | bytes 16416 | tf_op jit(solution)/shard_map/ppermute | solution.py:111
  38.1 0.0 all-to-all-done.own_ref
  38.1 0.9 %broadcast_in_dim.5 = bf16[16,2,64,128]{3,2,1,0:T(8,128)(2,1)} broadcast(bf16[2,64,128]{2,1,0:T(8,128)(2,1)S(1)} %pad_maximum_fusion), dimensions={1,2,3} | broadcast | bytes 557056 | tf_op jit(solution)/shard_map/broadcast_in_dim | solution.py:115
  39.0 0.0 copy-start.2
  39.0 6.9 %all-to-all-start.1 = ((bf16[16,2,64,128]{3,2,1,0:T(8,128)(2,1)}), bf16[16,2,64,128]{3,2,1,0:T(8,128)(2,1)S(1)}, u32[]{:S(2)}, u32[]{:S(2)}) async-start(bf16[16,2,64,128]{3,2,1,0:T(8,128)(2,1)} %broadcast_in_dim.5), calls=%async_computation.1 | async-start | bytes 1048576 | tf_op jit(solution)/shard_map/all_to_all | solution.py:115
  45.9 2.0 %collective-permute-start.1 = (bf16[8,128,128]{2,1,0:T(8,128)(2,1)S(1)}, bf16[8,128,128]{2,1,0:T(8,128)(2,1)S(1)}, u32[]{:S(2)}, u32[]{:S(2)}) collective-permute-start(bf16[8,128,128]{2,1,0:T(8,128)(2,1)S(1)} %all-to-all-done.own_ref), channel_id=1, source_target_pairs={{0,4},{4,0},{1,5},{5,1},{2,6},{6,2},{3,7},{7,3},{8,12},{12,8},{9,1... | collective-permute-start | bytes 786440 | tf_op jit(solution)/shard_map/ppermute | solution.py:114
  47.9 5.1 %collective-permute-done.1.near_ref = bf16[8,128,128]{2,1,0:T(8,128)(2,1)S(1)} collective-permute-done((bf16[8,128,128]{2,1,0:T(8,128)(2,1)S(1)}, bf16[8,128,128]{2,1,0:T(8,128)(2,1)S(1)}, u32[]{:S(2)}, u32[]{:S(2)}) %collective-permute-start.1) | collective-permute-done | bytes 262176 | tf_op jit(solution)/shard_map/ppermute | solution.py:114
  53.0 1.9 %all-to-all-done.1.left_ref = bf16[16,2,64,128]{3,2,1,0:T(8,128)(2,1)S(1)} async-done(((bf16[16,2,64,128]{3,2,1,0:T(8,128)(2,1)}), bf16[16,2,64,128]{3,2,1,0:T(8,128)(2,1)S(1)}, u32[]{:S(2)}, u32[]{:S(2)}) %all-to-all-start.1) | async-done | bytes 524320 | tf_op jit(solution)/shard_map/all_to_all | solution.py:115
  54.9 0.0 copy-done.2
  54.9 3.6 %pair_block.1 = bf16[256,512]{1,0:T(8,128)(2,1)S(1)} custom-call(bf16[8,128,128]{2,1,0:T(8,128)(2,1)S(1)} %all-to-all-done.own_ref, bf16[8,128,128]{2,1,0:T(8,128)(2,1)S(1)} %collective-permute-done.1.near_ref, bf16[16,2,64,128]{3,2,1,0:T(8,128)(2,1)S(1)} %all-to-all-done.1.left_ref, bf16[1024,128]{1,0:T(8,128)(2,1)S(1)} %copy-done.2), custom_call_target="tpu_custom_call" | custom-call | tf_op jit(solution)/shard_map/pair_block/pallas_call | solution.py:117
  58.5 21.6 %all_to_all.15 = bf16[32,8,512]{2,1,0:T(8,128)(2,1)S(1)} all-to-all(bf16[32,8,512]{2,1,0:T(8,128)(2,1)S(1)} %bitcast.11), channel_id=1, replica_groups=mesh['y'=4,'x'=4,'zq'=4,'zp'=2,'zh'=2,'core'=2] {'y','x','core'}, dimensions={0} | all-to-all | bytes 524288 | tf_op jit(solution)/shard_map/all_to_all | solution.py:130
  80.1 0.0 copy-start.7
  80.1 0.7 copy-done.7
  80.7 0.7 sum_and_bias.1
  (1 shorter events, 0.0 us)
Async XLA Ops:
  0.8 0.7 copy-start.4
  0.8 0.7 copy-start.3
  0.9 0.7 copy-start.5
  1.5 1.0 %copy-start = (bf16[128,4,256]{2,1,0:T(4,128)(2,1)S(1)}, bf16[128,4,256]{2,1,0:T(4,128)(2,1)}, u32[]{:S(2)}) copy-start(bf16[128,4,256]{2,1,0:T(4,128)(2,1)} %x_ref.3) | copy-start | bytes 786436
  4.4 15.8 %copy-start.8 = (bf16[256,32]{0,1:T(8,128)(2,1)S(1)}, bf16[256,32]{0,1:T(8,128)(2,1)}, u32[]{:S(2)}) copy-start(bf16[256,32]{0,1:T(8,128)(2,1)} %param.12) | copy-start | bytes 49156
  4.4 15.9 %copy-start.1 = (bf16[128,4,256]{2,1,0:T(4,128)(2,1)S(1)}, bf16[128,4,256]{2,1,0:T(4,128)(2,1)}, u32[]{:S(2)}) copy-start(bf16[128,4,256]{2,1,0:T(4,128)(2,1)} %x_ref.3) | copy-start | bytes 786436
  4.4 33.7 %all-to-all-start = ((bf16[8,128,128]{2,1,0:T(8,128)(2,1)}), bf16[8,128,128]{2,1,0:T(8,128)(2,1)S(1)}, u32[]{:S(2)}, u32[]{:S(2)}) async-start(bf16[8,128,128]{2,1,0:T(8,128)(2,1)} %broadcast_in_dim.4), calls=%async_computation | async-start | bytes 524288 | tf_op jit(solution)/shard_map/all_to_all | solution.py:110
  20.3 0.7 copy-start.6
  22.0 16.1 %collective-permute-start = (bf16[64,128]{1,0:T(8,128)(2,1)S(1)}, bf16[64,128]{1,0:T(8,128)(2,1)S(1)}, u32[]{:S(2)}, u32[]{:S(2)}) collective-permute-start(bf16[64,128]{1,0:T(8,128)(2,1)S(1)} %get-tuple-element.10), channel_id=1, source_target_pairs={{0,2},{2,0},{1,3},{3,1},{4,6},{6,4},{5,7},{7,5},{8,10},{10,8},{9,1... | collective-permute-start | bytes 49160 | tf_op jit(solution)/shard_map/ppermute | solution.py:111
  39.0 15.9 %copy-start.2 = (bf16[1024,128]{1,0:T(8,128)(2,1)S(1)}, bf16[1024,128]{1,0:T(8,128)(2,1)}, u32[]{:S(2)}) copy-start(bf16[1024,128]{1,0:T(8,128)(2,1)} %map_ref.1) | copy-start | bytes 786436
  39.0 15.9 %all-to-all-start.1 = ((bf16[16,2,64,128]{3,2,1,0:T(8,128)(2,1)}), bf16[16,2,64,128]{3,2,1,0:T(8,128)(2,1)S(1)}, u32[]{:S(2)}, u32[]{:S(2)}) async-start(bf16[16,2,64,128]{3,2,1,0:T(8,128)(2,1)} %broadcast_in_dim.5), calls=%async_computation.1 | async-start | bytes 1048576 | tf_op jit(solution)/shard_map/all_to_all | solution.py:115
  45.9 7.1 %collective-permute-start.1 = (bf16[8,128,128]{2,1,0:T(8,128)(2,1)S(1)}, bf16[8,128,128]{2,1,0:T(8,128)(2,1)S(1)}, u32[]{:S(2)}, u32[]{:S(2)}) collective-permute-start(bf16[8,128,128]{2,1,0:T(8,128)(2,1)S(1)} %all-to-all-done.own_ref), channel_id=1, source_target_pairs={{0,4},{4,0},{1,5},{5,1},{2,6},{6,2},{3,7},{7,3},{8,12},{12,8},{9,1... | collective-permute-start | bytes 786440 | tf_op jit(solution)/shard_map/ppermute | solution.py:114
  80.1 0.7 copy-start.7

commit v2 on v1

v2 whole, which is shorter than its diff:
```python
import jax
import jax.numpy as jnp
from jax import lax
from jax.experimental import pallas as pl
from jax.experimental.pallas import tpu as pltpu
from jax.sharding import Mesh, PartitionSpec as P

F32 = jnp.float32
BF16 = jnp.bfloat16
AXES = ("y", "x", "zu", "zv", "zp", "zh", "core")
RING = ("zu", "zv", "zp", "zh")
NT = (((1,), (1,)), ((), ()))


def projection_kernel(x_hbm, gain_hbm, offset_hbm, left_hbm, left_bias_hbm, right_hbm, right_bias_hbm, right_out, left_out, far_ref, x_ref, gain_ref, offset_ref, left_ref, left_bias_ref, right_ref, right_bias_ref, sems):
    pairs = (
        (x_hbm, x_ref),
        (gain_hbm, gain_ref),
        (offset_hbm, offset_ref),
        (left_hbm, left_ref),
        (left_bias_hbm, left_bias_ref),
        (right_hbm, right_ref),
        (right_bias_hbm, right_bias_ref),
    )
    copies = [pltpu.make_async_copy(src, dst, sems.at[k]) for k, (src, dst) in enumerate(pairs)]
    for copy in copies:
        copy.start()
    for copy in copies:
        copy.wait()
    x = x_ref[...].astype(F32)
    centre = jnp.mean(x, axis=-1, keepdims=True)
    shifted = x - centre
    spread = jnp.mean(shifted * shifted, axis=-1, keepdims=True)
    normed = shifted * lax.rsqrt(spread + 1e-05) * gain_ref[...].reshape(1, 1, 256)
    normed = normed + offset_ref[...].reshape(1, 1, 256)
    both = jnp.concatenate([right_ref[...], left_ref[...]], axis=0)
    bias = jnp.concatenate([right_bias_ref[...], left_bias_ref[...]], axis=1)
    bias = jnp.broadcast_to(bias, (128, 64)).T
    rows = [
        (
            lax.dot_general(both, normed[:, r, :].astype(BF16), NT, preferred_element_type=F32)
            + bias
        ).astype(BF16)
        for r in range(4)
    ]
    right_out[...] = jnp.concatenate([row[:32] for row in rows], axis=0)
    far_ref[:128, :] = right_out[...]
    first = jnp.concatenate([rows[0][32:], rows[1][32:]], axis=0)
    second = jnp.concatenate([rows[2][32:], rows[3][32:]], axis=0)
    low = lax.axis_index("zh") == 0
    left_out[...] = jnp.where(low, first, second)
    far_ref[128:, :] = jnp.where(low, second, first)


def arrange_kernel(left_ref, right_ref, far_ref, below_ref, above_ref, left_out, right_out):
    half, upper = lax.axis_index("zh"), lax.axis_index("zu")
    own, far = left_ref[...], far_ref[128:, :]
    first, second = jnp.where(half == 0, own, far), jnp.where(half == 0, far, own)
    for to in range(16):
        left_out[to, 0] = first
        left_out[to, 1] = second
    here = half * 2 + upper
    right_out[here] = right_ref[...]
    right_out[(here + 2) % 4] = far_ref[:128, :]
    right_out[(here + 3) % 4] = below_ref[...]
    right_out[(here + 1) % 4] = above_ref[...]


def pair_kernel(near0, near1, near2, near3, left_ref, map_ref, bias_ref, out_ref, bias_out, a32, a16, x16, wide_ref, res):
    place = lax.axis_index("zv") * 2 + lax.axis_index("zp")
    for yx in range(16):
        for block in range(2):
            for ii in range(2):
                a32[pl.ds(block * 1024 + yx * 2 + ii, 32, stride=32), :] = left_ref[
                    yx, block, ii * 32 : ii * 32 + 32, :
                ].astype(F32)
    for block in range(2):
        a16[:, block * 128 : block * 128 + 128] = a32[block * 1024 : block * 1024 + 1024, :].astype(BF16)
    bias_out[...] = bias_ref[...]
    wide_ref[...] = jnp.zeros_like(wide_ref)
    for c in range(32):
        for r in range(4):
            wide_ref[c * 128 + r * 32 : c * 128 + r * 32 + 32, r * 128 : r * 128 + 128] = map_ref[
                c * 32 : c * 32 + 32, :
            ]
    for k, near in ((0, near0), (-1, near1), (1, near2), (2, near3)):
        for zu in range(2):
            zl = zu * 4 + (place + k + 4) % 4
            row = pl.multiple_of(zl * 32, 32)
            right = jnp.concatenate([near[zu], near[2 + zu]], axis=1)
            outer = lax.dot_general(a16[...], right, NT, preferred_element_type=F32).astype(BF16)
            for c in range(32):
                x16[pl.ds(row, 32), c * 128 : c * 128 + 128] = outer[c * 32 : c * 32 + 32, :]
    total = jnp.dot(x16[...], wide_ref[...], preferred_element_type=F32) * (1.0 / 512)
    for r in range(4):
        res[r * 256 : r * 256 + 256, :] = total[:, r * 128 : r * 128 + 128]
    for r in range(4):
        for i in range(0, 32, 2):
            rows = [res[pl.ds(r * 256 + i + k, 8, stride=32), :] for k in range(2)]
            out_ref[i * 8 : i * 8 + 16, r * 128 : r * 128 + 128] = jnp.concatenate(rows, axis=0).astype(BF16)


def final_kernel(parts_ref, bias_ref, out_ref, rows):
    parts = parts_ref[...].astype(F32).reshape(16, 2, 8, 512)
    summed = (parts[:, 0] + parts[:, 1]).reshape(128, 512)
    for r in range(4):
        rows[pl.ds(r, 128, stride=4), :] = summed[:, r * 128 : r * 128 + 128] + bias_ref[...]
    out_ref[...] = rows[...].astype(BF16)


def params(mib):
    return pltpu.CompilerParams(vmem_limit_bytes=mib * 2**20)


def shape(*dims, dtype=BF16):
    return jax.ShapeDtypeStruct(dims, dtype)


def from_ring(value, step):
    place = [z % 8 * 2 + z // 8 for z in range(16)]
    return lax.ppermute(value, RING, [(place[(z + step) % 16], place[z]) for z in range(16)])


def local(x, gain, offset, first, first_bias, second, second_bias, mapping, final_bias):
    operands = (
        x,
        gain.reshape(1, 256),
        offset.reshape(1, 256),
        first.T,
        first_bias.reshape(1, 32),
        second.T,
        second_bias.reshape(1, 32),
    )
    right, left, far = pl.pallas_call(
        projection_kernel,
        out_shape=(shape(128, 128), shape(64, 128), shape(192, 128)),
        in_specs=[pl.BlockSpec(memory_space=pltpu.HBM)] * 7,
        scratch_shapes=[pltpu.VMEM(a.shape, a.dtype) for a in operands] + [pltpu.SemaphoreType.DMA((7,))],
        compiler_params=params(60),
        name="projections",
    )(*operands)
    far = from_ring(far, 8)
    below, above = from_ring(right, -4), from_ring(right, 4)
    left, right = pl.pallas_call(
        arrange_kernel,
        out_shape=(shape(16, 2, 64, 128), shape(4, 128, 128)),
        compiler_params=params(16),
        name="arrange",
    )(left, right, far, below, above)
    left = lax.all_to_all(left, ("y", "x"), 0, 0)
    near = [from_ring(right, step) for step in (-1, 1, 2)]

    parts, bias = pl.pallas_call(
        pair_kernel,
        out_shape=(shape(256, 512), shape(1, 128, dtype=F32)),
        scratch_shapes=[
            pltpu.VMEM((2048, 128), F32),
            pltpu.VMEM((1024, 256), BF16),
            pltpu.VMEM((256, 4096), BF16),
            pltpu.VMEM((4096, 512), BF16),
            pltpu.VMEM((1024, 128), F32),
        ],
        compiler_params=params(20),
        name="pair_block",
    )(right, *near, left, mapping, final_bias.reshape(1, 128))
    parts = lax.all_to_all(parts.reshape(32, 8, 512), ("y", "x", "core"), 0, 0)
    out = pl.pallas_call(
        final_kernel,
        out_shape=shape(512, 128),
        scratch_shapes=[pltpu.VMEM((512, 128), F32)],
        compiler_params=params(16),
        name="sum_and_bias",
    )(parts.reshape(256, 512), bias)
    return out.reshape(1, 512, 128)


def solution(mesh):
    fine = Mesh(mesh.devices.reshape(4, 4, 2, 2, 2, 2, 2), AXES)
    placed = (P(("zh", "core"), ("y", "x", "zu", "zv", "zp"), None),) + (P(),) * 8
    return jax.shard_map(
        local, mesh=fine, in_specs=placed, out_specs=P(AXES, None, None), check_vma=False
    )
```

time: 82 us -> 77.2 us (0.941)
  waiting for transfers between devices: 10.9 us -> 6.58 us
  starting transfers between devices: 36.7 us -> 41 us
  local copies, waits for them, and re-layouts: 5.53 us -> 1.49 us
  blocking collectives: 21.6 us -> 19.2 us
  Pallas kernels: 6.57 us -> 8.33 us
    ppermute x2 -> x6, starting transfers between devices: 14.1 us -> 34.1 us  [from_ring(): lax.ppermute(value, RING, [(place[(z + step) % 16], place[z]) for z in ra...]
    all_to_all x2 -> x1, starting transfers between devices: 22.7 us -> 6.89 us  [local(): left = lax.all_to_all(left, ('y', 'x'), 0, 0)]
    ppermute x2 -> x6, waiting for transfers between devices: 9.06 us -> 6.58 us  [from_ring(): lax.ppermute(value, RING, [(place[(z + step) % 16], place[z]) for z in ra...]
    unnamed x20 -> x8, local copies, waits for them, and re-layouts: 3.89 us -> 1.49 us
    all_to_all x1, blocking collectives: 21.6 us -> 19.2 us  [local(): parts = lax.all_to_all(parts.reshape(32, 8, 512), ('y', 'x', 'core'), 0, 0)]
    all_to_all x2 -> x1, waiting for transfers between devices: 1.88 us -> 0.01 us  [local(): left = lax.all_to_all(left, ('y', 'x'), 0, 0)]
    pallas_call x4, Pallas kernels: 6.57 us -> 8.33 us  [the longest x1 3.9 us: local(): pl.pallas_call(pair_kernel, out_shape=(shape(256, 512), shape(1, 128, dty...]
    broadcast_in_dim x2 -> x0, local copies, waits for them, and re-layouts: 1.64 us -> none  [the longest x1 0.91 us: local(): jnp.broadcast_to(left[None], (16, 2, 64, 128))]
  transfers between devices with their start and end apart: 4 -> 7, of which waited for: 3 -> 3; matrix products, arithmetic and copies ran while one was open for 0% -> 0% of each run, Pallas kernels for 1% -> 0%
where the time goes in v2:
time: 77.2 us; the launch traced here: 76.7 us
  starting transfers between devices  41 us (53%)
  blocking collectives  19.2 us (25%)
  Pallas kernels  8.33 us (11%)
  waiting for transfers between devices  6.58 us (9%)
  local copies, waits for them, and re-layouts  1.49 us (2%)
    ppermute x6, starting transfers between devices, from_ring(): lax.ppermute(value, RING, [(place[(z + step) % 16], place[z]) for z in ra...  34.1 us
    all_to_all x1, blocking collectives, local(): parts = lax.all_to_all(parts.reshape(32, 8, 512), ('y', 'x', 'core'), 0, 0)  19.2 us
    all_to_all x1, starting transfers between devices, local(): left = lax.all_to_all(left, ('y', 'x'), 0, 0)  6.89 us
    ppermute x6, waiting for transfers between devices, from_ring(): lax.ppermute(value, RING, [(place[(z + step) % 16], place[z]) for z in ra...  6.58 us
    pallas_call x1, Pallas kernels, local(): pl.pallas_call(pair_kernel, out_shape=(shape(256, 512), shape(1, 128, dty...  3.9 us
    pallas_call x1, Pallas kernels, local(): pl.pallas_call(projection_kernel, out_shape=(shape(128, 128), shape(64, 1...  2.79 us
  transfers between devices with their start and end apart: 7, of which 3 were waited for; matrix products, arithmetic and copies ran while one was open for 0% of the time, Pallas kernels for 0%

profile of v2, /device:TPU:1, one launch (start us, length us, event | category | flops | bytes accessed | tf_op | source)
XLA Modules:
  0.0 76.7 jit_solution(14832300456848026847)
XLA Ops:
  0.0 2.8 %projections.1 = (bf16[128,128]{1,0:T(8,128)(2,1)}, bf16[64,128]{1,0:T(8,128)(2,1)}, bf16[192,128]{1,0:T(8,128)(2,1)}) custom-call(bf16[128,4,256]{2,1,0:T(4,128)(2,1)} %x_hbm.1, f32[1,256]{1,0:T(1,128)} %bitcast.15, f32[1,256]{1,0:T(1,128)} %bitcast.16, bf16[32,256]{1,0:T(8,128)(2,1)} %bitcast.13, f32[1,32]{1,0:T(1,128)} %bitcast.17, ...), custom_call_target="tpu_custom_call" | custom-call | tf_op jit(solution)/shard_map/projections/pallas_call | solution.py:134
  2.8 16.3 %collective-permute-start = (bf16[192,128]{1,0:T(8,128)(2,1)}, bf16[192,128]{1,0:T(8,128)(2,1)S(1)}, u32[]{:S(2)}, u32[]{:S(2)}) collective-permute-start(bf16[192,128]{1,0:T(8,128)(2,1)} %get-tuple-element.14), channel_id=1, source_target_pairs={{2,0},{6,4},{10,8},{14,12},{18,16},{22,20},{26,24},{30,28},{0,2},{... | collective-permute-start | bytes 147464 | tf_op jit(solution)/shard_map/ppermute | solution.py:121
  19.1 1.9 %collective-permute-start.2 = (bf16[128,128]{1,0:T(8,128)(2,1)}, bf16[128,128]{1,0:T(8,128)(2,1)S(1)}, u32[]{:S(2)}, u32[]{:S(2)}) collective-permute-start(bf16[128,128]{1,0:T(8,128)(2,1)} %get-tuple-element.13.right_ref), channel_id=1, source_target_pairs={{16,0},{20,4},{24,8},{28,12},{2,16},{6,20},{10,24},{14,28},{18,2},... | collective-permute-start | bytes 98312 | tf_op jit(solution)/shard_map/ppermute | solution.py:121
  21.0 7.3 %collective-permute-start.1 = (bf16[128,128]{1,0:T(8,128)(2,1)}, bf16[128,128]{1,0:T(8,128)(2,1)S(1)}, u32[]{:S(2)}, u32[]{:S(2)}) collective-permute-start(bf16[128,128]{1,0:T(8,128)(2,1)} %get-tuple-element.13.right_ref), channel_id=1, source_target_pairs={{18,0},{22,4},{26,8},{30,12},{0,16},{4,20},{8,24},{12,28},{16,2},{... | collective-permute-start | bytes 98312 | tf_op jit(solution)/shard_map/ppermute | solution.py:121
  28.3 0.0 collective-permute-done.2.above_ref
  28.3 1.6 %collective-permute-done.1.below_ref = bf16[128,128]{1,0:T(8,128)(2,1)S(1)} collective-permute-done((bf16[128,128]{1,0:T(8,128)(2,1)}, bf16[128,128]{1,0:T(8,128)(2,1)S(1)}, u32[]{:S(2)}, u32[]{:S(2)}) %collective-permute-start.1) | collective-permute-done | bytes 32800 | tf_op jit(solution)/shard_map/ppermute | solution.py:121
  29.9 0.0 collective-permute-done.far_ref
  29.9 0.0 copy-start.1
  29.9 0.8 copy-done.1
  30.6 0.0 copy-start.2
  30.6 0.7 copy-done.2
  31.4 0.9 %arrange.1 = (bf16[16,2,64,128]{3,2,1,0:T(8,128)(2,1)}, bf16[4,128,128]{2,1,0:T(8,128)(2,1)S(1)}) custom-call(bf16[64,128]{1,0:T(8,128)(2,1)S(1)} %copy-done.2, bf16[128,128]{1,0:T(8,128)(2,1)S(1)} %copy-done.1, bf16[192,128]{1,0:T(8,128)(2,1)S(1)} %collective-permute-done.far_ref, bf16[128,128]{1,0:T(8,128)(2,1)S(1)} %collective-permute-done.1.below_ref, ...), custom_call_target="tpu_custom_call" | custom-call | tf_op jit(solution)/shard_map/arrange/pallas_call | solution.py:144
  32.3 0.0 copy-start
  32.3 6.9 %all-to-all-start = ((bf16[16,2,64,128]{3,2,1,0:T(8,128)(2,1)}), bf16[16,2,64,128]{3,2,1,0:T(8,128)(2,1)S(1)}, u32[]{:S(2)}, u32[]{:S(2)}) async-start(bf16[16,2,64,128]{3,2,1,0:T(8,128)(2,1)} %get-tuple-element.16), calls=%async_computation | async-start | bytes 1048576 | tf_op jit(solution)/shard_map/all_to_all | solution.py:150
  39.2 0.0 copy-start.3
  39.2 3.1 %collective-permute-start.5 = (bf16[4,128,128]{2,1,0:T(8,128)(2,1)S(1)}, bf16[4,128,128]{2,1,0:T(8,128)(2,1)S(1)}, u32[]{:S(2)}, u32[]{:S(2)}) collective-permute-start(bf16[4,128,128]{2,1,0:T(8,128)(2,1)S(1)} %get-tuple-element.15.near0), channel_id=1, source_target_pairs={{8,0},{12,4},{16,8},{20,12},{24,16},{28,20},{2,24},{6,28},{10,2},{... | collective-permute-start | bytes 393224 | tf_op jit(solution)/shard_map/ppermute | solution.py:121
  42.2 3.7 %collective-permute-start.4 = (bf16[4,128,128]{2,1,0:T(8,128)(2,1)S(1)}, bf16[4,128,128]{2,1,0:T(8,128)(2,1)S(1)}, u32[]{:S(2)}, u32[]{:S(2)}) collective-permute-start(bf16[4,128,128]{2,1,0:T(8,128)(2,1)S(1)} %get-tuple-element.15.near0), channel_id=1, source_target_pairs={{4,0},{8,4},{12,8},{16,12},{20,16},{24,20},{28,24},{2,28},{6,2},{1... | collective-permute-start | bytes 393224 | tf_op jit(solution)/shard_map/ppermute | solution.py:121
  45.9 1.9 %collective-permute-start.3 = (bf16[4,128,128]{2,1,0:T(8,128)(2,1)S(1)}, bf16[4,128,128]{2,1,0:T(8,128)(2,1)S(1)}, u32[]{:S(2)}, u32[]{:S(2)}) collective-permute-start(bf16[4,128,128]{2,1,0:T(8,128)(2,1)S(1)} %get-tuple-element.15.near0), channel_id=1, source_target_pairs={{30,0},{0,4},{4,8},{8,12},{12,16},{16,20},{20,24},{24,28},{28,2},{... | collective-permute-start | bytes 393224 | tf_op jit(solution)/shard_map/ppermute | solution.py:121
  47.9 0.0 collective-permute-done.5.near3
  47.9 2.3 %collective-permute-done.4.near2 = bf16[4,128,128]{2,1,0:T(8,128)(2,1)S(1)} collective-permute-done((bf16[4,128,128]{2,1,0:T(8,128)(2,1)S(1)}, bf16[4,128,128]{2,1,0:T(8,128)(2,1)S(1)}, u32[]{:S(2)}, u32[]{:S(2)}) %collective-permute-start.4) | collective-permute-done | bytes 131104 | tf_op jit(solution)/shard_map/ppermute | solution.py:121
  50.2 2.6 %collective-permute-done.3.near1 = bf16[4,128,128]{2,1,0:T(8,128)(2,1)S(1)} collective-permute-done((bf16[4,128,128]{2,1,0:T(8,128)(2,1)S(1)}, bf16[4,128,128]{2,1,0:T(8,128)(2,1)S(1)}, u32[]{:S(2)}, u32[]{:S(2)}) %collective-permute-start.3) | collective-permute-done | bytes 131104 | tf_op jit(solution)/shard_map/ppermute | solution.py:121
  52.9 0.0 all-to-all-done.left_ref
  52.9 0.0 copy-done
  52.9 0.0 copy-done.3
  52.9 3.9 %pair_block.1 = (bf16[256,512]{1,0:T(8,128)(2,1)S(1)}, f32[1,128]{1,0:T(1,128)S(1)}) custom-call(bf16[4,128,128]{2,1,0:T(8,128)(2,1)S(1)} %get-tuple-element.15.near0, bf16[4,128,128]{2,1,0:T(8,128)(2,1)S(1)} %collective-permute-done.3.near1, bf16[4,128,128]{2,1,0:T(8,128)(2,1)S(1)} %collective-permute-done.4.near2, ...), custom_call_target="tpu_custom_call" | custom-call | tf_op jit(solution)/shard_map/pair_block/pallas_call | solution.py:153
  56.8 19.2 %all_to_all.10 = bf16[32,8,512]{2,1,0:T(8,128)(2,1)S(1)} all-to-all(bf16[32,8,512]{2,1,0:T(8,128)(2,1)S(1)} %bitcast.11), channel_id=1, replica_groups=mesh['y'=4,'x'=4,'zu'=2,'zv'=2,'zp'=2,'zh'=2,'core'=2] {'y','x','core'}, dimensions={0} | all-to-all | bytes 524288 | tf_op jit(solution)/shard_map/all_to_all | solution.py:166
  76.0 0.7 sum_and_bias.1
Async XLA Ops:
  2.8 27.1 %collective-permute-start = (bf16[192,128]{1,0:T(8,128)(2,1)}, bf16[192,128]{1,0:T(8,128)(2,1)S(1)}, u32[]{:S(2)}, u32[]{:S(2)}) collective-permute-start(bf16[192,128]{1,0:T(8,128)(2,1)} %get-tuple-element.14), channel_id=1, source_target_pairs={{2,0},{6,4},{10,8},{14,12},{18,16},{22,20},{26,24},{30,28},{0,2},{... | collective-permute-start | bytes 147464 | tf_op jit(solution)/shard_map/ppermute | solution.py:121
  19.1 9.2 %collective-permute-start.2 = (bf16[128,128]{1,0:T(8,128)(2,1)}, bf16[128,128]{1,0:T(8,128)(2,1)S(1)}, u32[]{:S(2)}, u32[]{:S(2)}) collective-permute-start(bf16[128,128]{1,0:T(8,128)(2,1)} %get-tuple-element.13.right_ref), channel_id=1, source_target_pairs={{16,0},{20,4},{24,8},{28,12},{2,16},{6,20},{10,24},{14,28},{18,2},... | collective-permute-start | bytes 98312 | tf_op jit(solution)/shard_map/ppermute | solution.py:121
  21.0 8.9 %collective-permute-start.1 = (bf16[128,128]{1,0:T(8,128)(2,1)}, bf16[128,128]{1,0:T(8,128)(2,1)S(1)}, u32[]{:S(2)}, u32[]{:S(2)}) collective-permute-start(bf16[128,128]{1,0:T(8,128)(2,1)} %get-tuple-element.13.right_ref), channel_id=1, source_target_pairs={{18,0},{22,4},{26,8},{30,12},{0,16},{4,20},{8,24},{12,28},{16,2},{... | collective-permute-start | bytes 98312 | tf_op jit(solution)/shard_map/ppermute | solution.py:121
  29.9 0.8 copy-start.1
  30.6 0.7 copy-start.2
  32.3 20.6 %copy-start = (bf16[1024,128]{1,0:T(8,128)(2,1)S(1)}, bf16[1024,128]{1,0:T(8,128)(2,1)}, u32[]{:S(2)}) copy-start(bf16[1024,128]{1,0:T(8,128)(2,1)} %map_ref.1) | copy-start | bytes 786436
  32.3 20.6 %all-to-all-start = ((bf16[16,2,64,128]{3,2,1,0:T(8,128)(2,1)}), bf16[16,2,64,128]{3,2,1,0:T(8,128)(2,1)S(1)}, u32[]{:S(2)}, u32[]{:S(2)}) async-start(bf16[16,2,64,128]{3,2,1,0:T(8,128)(2,1)} %get-tuple-element.16), calls=%async_computation | async-start | bytes 1048576 | tf_op jit(solution)/shard_map/all_to_all | solution.py:150
  39.2 13.7 %copy-start.3 = (f32[128]{0:T(128)S(1)}, f32[128]{0:T(128)}, u32[]{:S(2)}) copy-start(f32[128]{0:T(128)} %param.17) | copy-start | bytes 1540
  39.2 8.7 %collective-permute-start.5 = (bf16[4,128,128]{2,1,0:T(8,128)(2,1)S(1)}, bf16[4,128,128]{2,1,0:T(8,128)(2,1)S(1)}, u32[]{:S(2)}, u32[]{:S(2)}) collective-permute-start(bf16[4,128,128]{2,1,0:T(8,128)(2,1)S(1)} %get-tuple-element.15.near0), channel_id=1, source_target_pairs={{8,0},{12,4},{16,8},{20,12},{24,16},{28,20},{2,24},{6,28},{10,2},{... | collective-permute-start | bytes 393224 | tf_op jit(solution)/shard_map/ppermute | solution.py:121
  42.2 8.0 %collective-permute-start.4 = (bf16[4,128,128]{2,1,0:T(8,128)(2,1)S(1)}, bf16[4,128,128]{2,1,0:T(8,128)(2,1)S(1)}, u32[]{:S(2)}, u32[]{:S(2)}) collective-permute-start(bf16[4,128,128]{2,1,0:T(8,128)(2,1)S(1)} %get-tuple-element.15.near0), channel_id=1, source_target_pairs={{4,0},{8,4},{12,8},{16,12},{20,16},{24,20},{28,24},{2,28},{6,2},{1... | collective-permute-start | bytes 393224 | tf_op jit(solution)/shard_map/ppermute | solution.py:121
  45.9 6.9 %collective-permute-start.3 = (bf16[4,128,128]{2,1,0:T(8,128)(2,1)S(1)}, bf16[4,128,128]{2,1,0:T(8,128)(2,1)S(1)}, u32[]{:S(2)}, u32[]{:S(2)}) collective-permute-start(bf16[4,128,128]{2,1,0:T(8,128)(2,1)S(1)} %get-tuple-element.15.near0), channel_id=1, source_target_pairs={{30,0},{0,4},{4,8},{8,12},{12,16},{16,20},{20,24},{24,28},{28,2},{... | collective-permute-start | bytes 393224 | tf_op jit(solution)/shard_map/ppermute | solution.py:121

commit v3 on v2

v3 whole, which is shorter than its diff:
```python
import jax
import jax.numpy as jnp
from jax import lax
from jax.experimental import pallas as pl
from jax.experimental.pallas import tpu as pltpu
from jax.sharding import Mesh, PartitionSpec as P

F32 = jnp.float32
BF16 = jnp.bfloat16
AXES = ("y", "x", "zu", "zv", "zp", "zh", "core")
SWAP = [(0, 1), (1, 0)]
NT = (((1,), (1,)), ((), ()))


def projection_kernel(
    x_hbm, gain_hbm, offset_hbm, left_hbm, left_bias_hbm, right_hbm, right_bias_hbm, map_hbm, bias_hbm,
    out_ref, map_out,
    x_ref, gain_ref, offset_ref, left_ref, left_bias_ref, right_ref, right_bias_ref, map_ref, bias_ref, sems,
):
    sources = (x_hbm, gain_hbm, offset_hbm, left_hbm, left_bias_hbm, right_hbm, right_bias_hbm, map_hbm, bias_hbm)
    targets = (x_ref, gain_ref, offset_ref, left_ref, left_bias_ref, right_ref, right_bias_ref, map_ref, bias_ref)
    copies = [
        pltpu.make_async_copy(src, dst, sems.at[k]) for k, (src, dst) in enumerate(zip(sources, targets))
    ]
    for copy in copies:
        copy.start()
    for copy in copies[:7]:
        copy.wait()
    x = x_ref[...].astype(F32)
    centre = jnp.mean(x, axis=-1, keepdims=True)
    shifted = x - centre
    spread = jnp.mean(shifted * shifted, axis=-1, keepdims=True)
    normed = shifted * lax.rsqrt(spread + 1e-05) * gain_ref[...].reshape(1, 1, 256)
    normed = normed + offset_ref[...].reshape(1, 1, 256)
    both = jnp.concatenate([right_ref[...], left_ref[...]], axis=0)
    bias = jnp.concatenate([right_bias_ref[...], left_bias_ref[...]], axis=1)
    bias = jnp.broadcast_to(bias, (128, 64)).T
    for r in range(4):
        rows = lax.dot_general(both, normed[:, r, :].astype(BF16), NT, preferred_element_type=F32)
        rows = (rows + bias).astype(BF16)
        out_ref[r * 32 : r * 32 + 32, :] = rows[:32]
        out_ref[128 + r * 32 : 160 + r * 32, :] = rows[32:]
    for copy in copies[7:]:
        copy.wait()
    map_out[:1024, :] = map_ref[...].astype(F32)
    map_out[1024:, :] = jnp.broadcast_to(bias_ref[...], (8, 128))


def split_kernel(got_ref, right_out, left_out):
    first = lax.axis_index("core") == 0
    for block in range(2):
        right = got_ref[block, :128, :]
        for to in range(16):
            right_out[to, block] = right
        for half in range(2):
            row = 128 + half * 64
            left_out[block, half * 32 : half * 32 + 32, :] = jnp.where(
                first, got_ref[block, row : row + 32, :], got_ref[block, row + 32 : row + 64, :]
            )


def pair_kernel(left_ref, right_ref, map_ref, out_ref, bias_out, a32, a16, x16, wide_ref, res):
    bias_out[...] = map_ref[1024:1025, :]
    for t in range(8):
        zl = t % 2 * 4 + t // 2 % 2 * 2 + t // 4
        for block in range(2):
            for half in range(2):
                a32[pl.ds(block * 512 + zl * 2 + half, 32, stride=16), :] = left_ref[
                    t, block, half * 32 : half * 32 + 32, :
                ].astype(F32)
    for block in range(2):
        a16[:, block * 128 : block * 128 + 128] = a32[block * 512 : block * 512 + 512, :].astype(BF16)
    wide_ref[...] = jnp.zeros_like(wide_ref)
    for c in range(32):
        for r in range(4):
            wide_ref[c * 128 + r * 32 : c * 128 + r * 32 + 32, r * 128 : r * 128 + 128] = map_ref[
                c * 32 : c * 32 + 32, :
            ].astype(BF16)
    for yx in range(16):
        right = jnp.concatenate([right_ref[yx, 0], right_ref[yx, 1]], axis=1)
        outer = lax.dot_general(a16[...], right, NT, preferred_element_type=F32).astype(BF16)
        for c in range(32):
            x16[yx * 16 : yx * 16 + 16, c * 128 : c * 128 + 128] = outer[c * 16 : c * 16 + 16, :]
    total = jnp.dot(x16[...], wide_ref[...], preferred_element_type=F32) * (1.0 / 512)
    for r in range(4):
        res[r * 256 : r * 256 + 256, :] = total[:, r * 128 : r * 128 + 128]
    for k in range(8):
        for half in range(2):
            to = half * 8 + k
            for r in range(4):
                rows = res[pl.ds(r * 256 + k * 2 + half, 16, stride=16), :]
                out_ref[to, :, r * 128 : r * 128 + 128] = rows.astype(BF16)


def final_kernel(parts_ref, bias_ref, out_ref, rows):
    for zl in range(8):
        summed = parts_ref[zl].astype(F32) + parts_ref[8 + zl].astype(F32)
        for r in range(4):
            rows[pl.ds(zl * 4 + r, 16, stride=32), :] = summed[:, r * 128 : r * 128 + 128] + bias_ref[...]
    out_ref[...] = rows[...].astype(BF16)


def params(mib):
    return pltpu.CompilerParams(vmem_limit_bytes=mib * 2**20)


def shape(*dims, dtype=BF16):
    return jax.ShapeDtypeStruct(dims, dtype)


def local(x, gain, offset, first, first_bias, second, second_bias, mapping, final_bias):
    operands = (
        x,
        gain.reshape(1, 256),
        offset.reshape(1, 256),
        first.T,
        first_bias.reshape(1, 32),
        second.T,
        second_bias.reshape(1, 32),
    )
    operands += (mapping, final_bias.reshape(1, 128))
    both, mapping = pl.pallas_call(
        projection_kernel,
        out_shape=(shape(256, 128), shape(1032, 128, dtype=F32)),
        in_specs=[pl.BlockSpec(memory_space=pltpu.HBM)] * 9,
        scratch_shapes=[pltpu.VMEM(a.shape, a.dtype) for a in operands] + [pltpu.SemaphoreType.DMA((9,))],
        compiler_params=params(60),
        name="projections",
    )(*operands)
    both = lax.all_gather(both, "core", axis=0)
    right, left0 = pl.pallas_call(
        split_kernel,
        out_shape=(shape(16, 2, 128, 128), shape(2, 64, 128)),
        compiler_params=params(16),
        name="split",
    )(both)
    right = lax.all_to_all(right, ("y", "x"), 0, 0)
    left = left0
    for axis in ("zu", "zv", "zp"):
        left = lax.all_gather(left, axis, axis=0)
    left = left.reshape(8, 2, 64, 128)

    parts, bias = pl.pallas_call(
        pair_kernel,
        out_shape=(shape(16, 16, 512), shape(1, 128, dtype=F32)),
        scratch_shapes=[
            pltpu.VMEM((1024, 128), F32),
            pltpu.VMEM((512, 256), BF16),
            pltpu.VMEM((256, 4096), BF16),
            pltpu.VMEM((4096, 512), BF16),
            pltpu.VMEM((1024, 128), F32),
        ],
        compiler_params=params(20),
        name="pair_block",
    )(left, right, mapping)
    parts = lax.all_to_all(parts, ("zh", "zu", "zv", "zp"), 0, 0)
    out = pl.pallas_call(
        final_kernel,
        out_shape=shape(512, 128),
        scratch_shapes=[pltpu.VMEM((512, 128), F32)],
        compiler_params=params(16),
        name="sum_and_bias",
    )(parts, bias)
    return out.reshape(1, 512, 128)


def solution(mesh):
    fine = Mesh(mesh.devices.reshape(4, 4, 2, 2, 2, 2, 2), AXES)
    placed = (P(("zh", "core"), ("y", "x", "zu", "zv", "zp"), None),) + (P(),) * 8
    return jax.shard_map(
        local, mesh=fine, in_specs=placed, out_specs=P(AXES, None, None), check_vma=False
    )
```

time: 77.2 us -> 70.5 us (0.913)
  the two profiles are of different devices: /device:TPU:1 before, /device:TPU:2 now
where the time goes in v3:
time: 70.5 us; the launch traced here: 70.2 us
  blocking collectives  53 us (75%)
  starting transfers between devices  9.35 us (13%)
  Pallas kernels  7.85 us (11%)
    all_to_all x1, blocking collectives, local(): parts = lax.all_to_all(parts, ('zh', 'zu', 'zv', 'zp'), 0, 0)  30.7 us
    all_gather x3, blocking collectives, local(): left = lax.all_gather(left, axis, axis=0)  20.2 us
    all_to_all x1, starting transfers between devices, local(): right = lax.all_to_all(right, ('y', 'x'), 0, 0)  9.35 us
    pallas_call x1, Pallas kernels, local(): pl.pallas_call(projection_kernel, out_shape=(shape(256, 128), shape(1032,...  3.02 us
    pallas_call x1, Pallas kernels, local(): pl.pallas_call(pair_kernel, out_shape=(shape(16, 16, 512), shape(1, 128,...  2.82 us
    all_gather x1, blocking collectives, local(): both = lax.all_gather(both, 'core', axis=0)  2.11 us
  transfers between devices with their start and end apart: 1, of which 0 were waited for; matrix products, arithmetic and copies ran while one was open for 0% of the time, Pallas kernels for 0%

profile of v3, /device:TPU:2, one launch (start us, length us, event | category | flops | bytes accessed | tf_op | source)
XLA Modules:
  0.0 70.2 jit_solution(4862553508718502634)
XLA Ops:
  0.0 3.0 %projections.1 = (bf16[256,128]{1,0:T(8,128)(2,1)}, f32[1032,128]{1,0:T(8,128)}) custom-call(bf16[128,4,256]{2,1,0:T(4,128)(2,1)} %x_hbm.1, f32[1,256]{1,0:T(1,128)} %bitcast.18, f32[1,256]{1,0:T(1,128)} %bitcast.19, bf16[32,256]{1,0:T(8,128)(2,1)} %bitcast.16, f32[1,32]{1,0:T(1,128)} %bitcast.20, bf16[32,256]{1,0:T(8,128)(2,1)} %bitcast.17, ...), custom_call_target="tpu_custom_call" | custom-call | tf_op jit(solution)/shard_map/projections/pallas_call | solution.py:122
  3.0 2.1 %all-gather = bf16[512,128]{1,0:T(8,128)(2,1)S(1)} all-gather(bf16[256,128]{1,0:T(8,128)(2,1)} %get-tuple-element.11), channel_id=2, replica_groups=mesh['y'=4,'x'=4,'zu'=2,'zv'=2,'zp'=2,'zh'=2,'core'=2] {'core'}, dimensions={0}, use_global_device_ids=true | all-gather | bytes 196608 | tf_op jit(solution)/shard_map/all_gather | solution.py:130
  5.1 1.2 %split.1 = (bf16[16,2,128,128]{3,2,1,0:T(8,128)(2,1)}, bf16[2,64,128]{2,1,0:T(8,128)(2,1)S(1)}) custom-call(bf16[2,256,128]{2,1,0:T(8,128)(2,1)S(1)} %bitcast.13), custom_call_target="tpu_custom_call" | custom-call | tf_op jit(solution)/shard_map/split/pallas_call | solution.py:131
  6.3 9.3 %all-to-all-start = ((bf16[16,2,128,128]{3,2,1,0:T(8,128)(2,1)}), bf16[16,2,128,128]{3,2,1,0:T(8,128)(2,1)S(1)}, u32[]{:S(2)}, u32[]{:S(2)}) async-start(bf16[16,2,128,128]{3,2,1,0:T(8,128)(2,1)} %get-tuple-element.13), calls=%async_computation | async-start | bytes 2097152 | tf_op jit(solution)/shard_map/all_to_all | solution.py:137
  15.7 0.0 copy-start
  15.7 8.6 %all-gather.1 = bf16[4,64,128]{2,1,0:T(8,128)(2,1)S(1)} all-gather(bf16[2,64,128]{2,1,0:T(8,128)(2,1)S(1)} %get-tuple-element.12), channel_id=3, replica_groups=mesh['y'=4,'x'=4,'zu'=2,'zv'=2,'zp'=2,'zh'=2,'core'=2] {'zu'}, dimensions={0}, use_global_device_ids=true | all-gather | bytes 98304 | tf_op jit(solution)/shard_map/all_gather | solution.py:140
  24.3 5.9 %all-gather.2 = bf16[4,2,64,128]{3,2,1,0:T(8,128)(2,1)S(1)} all-gather(bf16[2,2,64,128]{3,2,1,0:T(8,128)(2,1)S(1)} %bitcast.15), channel_id=4, replica_groups=mesh['y'=4,'x'=4,'zu'=2,'zv'=2,'zp'=2,'zh'=2,'core'=2] {'zv'}, dimensions={0}, use_global_device_ids=true | all-gather | bytes 196608 | tf_op jit(solution)/shard_map/all_gather | solution.py:140
  30.2 5.6 %all-gather.3 = bf16[4,2,2,64,128]{4,3,2,1,0:T(8,128)(2,1)S(1)} all-gather(bf16[2,2,2,64,128]{4,3,2,1,0:T(8,128)(2,1)S(1)} %bitcast.14), channel_id=5, replica_groups=mesh['y'=4,'x'=4,'zu'=2,'zv'=2,'zp'=2,'zh'=2,'core'=2] {'zp'}, dimensions={0}, use_global_device_ids=true | all-gather | bytes 393216 | tf_op jit(solution)/shard_map/all_gather | solution.py:140
  35.9 0.0 all-to-all-done.right_ref
  35.9 0.0 copy-done
  35.9 2.8 %pair_block.1 = (bf16[16,16,512]{2,1,0:T(8,128)(2,1)S(1)}, f32[1,128]{1,0:T(1,128)S(1)}) custom-call(bf16[8,2,64,128]{3,2,1,0:T(8,128)(2,1)S(1)} %bitcast.12, bf16[16,2,128,128]{3,2,1,0:T(8,128)(2,1)S(1)} %all-to-all-done.right_ref, f32[1032,128]{1,0:T(8,128)S(1)} %copy-done), custom_call_target="tpu_custom_call" | custom-call | tf_op jit(solution)/shard_map/pair_block/pallas_call | solution.py:143
  38.7 30.7 %all_to_all.10.parts_ref = bf16[16,16,512]{2,1,0:T(8,128)(2,1)S(1)} all-to-all(bf16[16,16,512]{2,1,0:T(8,128)(2,1)S(1)} %get-tuple-element.15), channel_id=1, replica_groups=mesh['y'=4,'x'=4,'zu'=2,'zv'=2,'zp'=2,'zh'=2,'core'=2] {'zh','zu','zv','..., dimensions={0} | all-to-all | bytes 524288 | tf_op jit(solution)/shard_map/all_to_all | solution.py:156
  69.4 0.8 %sum_and_bias.1 = bf16[512,128]{1,0:T(8,128)(2,1)} custom-call(bf16[16,16,512]{2,1,0:T(8,128)(2,1)S(1)} %all_to_all.10.parts_ref, f32[1,128]{1,0:T(1,128)S(1)} %get-tuple-element.16.bias_ref), custom_call_target="tpu_custom_call" | custom-call | tf_op jit(solution)/shard_map/sum_and_bias/pallas_call | solution.py:157
Async XLA Ops:
  6.3 29.5 %all-to-all-start = ((bf16[16,2,128,128]{3,2,1,0:T(8,128)(2,1)}), bf16[16,2,128,128]{3,2,1,0:T(8,128)(2,1)S(1)}, u32[]{:S(2)}, u32[]{:S(2)}) async-start(bf16[16,2,128,128]{3,2,1,0:T(8,128)(2,1)} %get-tuple-element.13), calls=%async_computation | async-start | bytes 2097152 | tf_op jit(solution)/shard_map/all_to_all | solution.py:137
  15.7 20.2 %copy-start = (f32[1032,128]{1,0:T(8,128)S(1)}, f32[1032,128]{1,0:T(8,128)}, u32[]{:S(2)}) copy-start(f32[1032,128]{1,0:T(8,128)} %get-tuple-element.14.map_ref) | copy-start | bytes 1585156

commit v4 on v3

v4 whole, which is shorter than its diff:
```python
import jax
import jax.numpy as jnp
from jax import lax
from jax.experimental import pallas as pl
from jax.experimental.pallas import tpu as pltpu
from jax.sharding import Mesh, PartitionSpec as P

F32 = jnp.float32
BF16 = jnp.bfloat16
AXES = ("y", "x", "zu", "zv", "zp", "zh", "core")
SWAP = [(0, 1), (1, 0)]
NT = (((1,), (1,)), ((), ()))


def projection_kernel(
    x_hbm, gain_hbm, offset_hbm, left_hbm, left_bias_hbm, right_hbm, right_bias_hbm, map_hbm, bias_hbm,
    right_out, left_out, map_out,
    x_ref, gain_ref, offset_ref, left_ref, left_bias_ref, right_ref, right_bias_ref, map_ref, bias_ref, sems,
):
    sources = (x_hbm, gain_hbm, offset_hbm, left_hbm, left_bias_hbm, right_hbm, right_bias_hbm, map_hbm, bias_hbm)
    targets = (x_ref, gain_ref, offset_ref, left_ref, left_bias_ref, right_ref, right_bias_ref, map_ref, bias_ref)
    copies = [
        pltpu.make_async_copy(src, dst, sems.at[k]) for k, (src, dst) in enumerate(zip(sources, targets))
    ]
    for copy in copies:
        copy.start()
    source = lax.broadcasted_iota(jnp.int32, (512, 512), 0)
    target = lax.broadcasted_iota(jnp.int32, (512, 512), 1)
    move = (source == target % 128 * 4 + target // 128).astype(F32).astype(BF16)
    for copy in copies[1:7]:
        copy.wait()
    both = jnp.concatenate([right_ref[...], left_ref[...]], axis=0)
    bias = jnp.concatenate([right_bias_ref[...], left_bias_ref[...]], axis=1)
    bias = jnp.broadcast_to(bias, (128, 64)).T
    copies[0].wait()
    x = x_ref[...].astype(F32).reshape(512, 256)
    centre = jnp.mean(x, axis=-1, keepdims=True)
    shifted = x - centre
    spread = jnp.mean(shifted * shifted, axis=-1, keepdims=True)
    normed = shifted * lax.rsqrt(spread + 1e-05) * gain_ref[...] + offset_ref[...]
    rows = lax.dot_general(both, normed.astype(BF16), NT, preferred_element_type=F32)
    rows = (rows + jnp.concatenate([bias] * 4, axis=1)).astype(BF16)
    rows = jnp.dot(rows, move, preferred_element_type=F32).astype(BF16)
    for r in range(4):
        for to in range(16):
            right_out[to, r * 32 : r * 32 + 32, :] = rows[:32, r * 128 : r * 128 + 128]
        left_out[r * 32 : r * 32 + 32, :] = rows[32:, r * 128 : r * 128 + 128]
    for copy in copies[7:]:
        copy.wait()
    map_out[:1024, :] = map_ref[...].astype(F32)
    map_out[1024:, :] = jnp.broadcast_to(bias_ref[...], (8, 128))


def join_kernel(own_ref, other_ref, out_ref):
    here = lax.axis_index("zu")
    out_ref[here] = own_ref[...]
    out_ref[1 - here] = other_ref[...]


def pair_kernel(left_ref, right_ref, other_ref, map_ref, out_ref, bias_out, a32, a16, x16, wide_ref, res):
    bias_out[...] = map_ref[1024:1025, :]
    core = lax.axis_index("core")
    for block, source in enumerate((core, 1 - core)):
        for t in range(8):
            zl = t % 2 * 4 + t // 2 % 2 * 2 + t // 4
            for half in range(2):
                row = pl.multiple_of((half * 2 + core) * 32, 32)
                a32[pl.ds(block * 512 + zl * 2 + half, 32, stride=16), :] = left_ref[
                    source, t, pl.ds(row, 32), :
                ].astype(F32)
        a16[:, block * 128 : block * 128 + 128] = a32[block * 512 : block * 512 + 512, :].astype(BF16)
    wide_ref[...] = jnp.zeros_like(wide_ref)
    for c in range(32):
        for r in range(4):
            wide_ref[c * 128 + r * 32 : c * 128 + r * 32 + 32, r * 128 : r * 128 + 128] = map_ref[
                c * 32 : c * 32 + 32, :
            ].astype(BF16)
    for first in range(0, 16, 4):
        chips = range(first, first + 4)
        right = [jnp.concatenate([right_ref[yx], other_ref[yx]], axis=1) for yx in chips]
        right = jnp.concatenate(right, axis=0)
        outer = lax.dot_general(a16[...], right, NT, preferred_element_type=F32).astype(BF16)
        for k, yx in enumerate(chips):
            for c in range(32):
                x16[yx * 16 : yx * 16 + 16, c * 128 : c * 128 + 128] = outer[
                    c * 16 : c * 16 + 16, k * 128 : k * 128 + 128
                ]
    total = jnp.dot(x16[...], wide_ref[...], preferred_element_type=F32) * (1.0 / 512)
    for r in range(4):
        res[r * 256 : r * 256 + 256, :] = total[:, r * 128 : r * 128 + 128]
    for k in range(8):
        for half in range(2):
            to = half * 8 + k
            for r in range(4):
                rows = res[pl.ds(r * 256 + k * 2 + half, 16, stride=16), :]
                out_ref[to, :, r * 128 : r * 128 + 128] = rows.astype(BF16)


def final_kernel(parts_ref, bias_ref, out_ref, rows):
    for zl in range(8):
        summed = parts_ref[zl].astype(F32) + parts_ref[8 + zl].astype(F32)
        for r in range(4):
            rows[pl.ds(zl * 4 + r, 16, stride=32), :] = summed[:, r * 128 : r * 128 + 128] + bias_ref[...]
    out_ref[...] = rows[...].astype(BF16)


def params(mib):
    return pltpu.CompilerParams(vmem_limit_bytes=mib * 2**20)


def shape(*dims, dtype=BF16):
    return jax.ShapeDtypeStruct(dims, dtype)


def local(x, gain, offset, first, first_bias, second, second_bias, mapping, final_bias):
    operands = (
        x,
        gain.reshape(1, 256),
        offset.reshape(1, 256),
        first.T,
        first_bias.reshape(1, 32),
        second.T,
        second_bias.reshape(1, 32),
    )
    operands += (mapping, final_bias.reshape(1, 128))
    right, left, mapping = pl.pallas_call(
        projection_kernel,
        out_shape=(shape(16, 128, 128), shape(128, 128), shape(1032, 128, dtype=F32)),
        in_specs=[pl.BlockSpec(memory_space=pltpu.HBM)] * 9,
        scratch_shapes=[pltpu.VMEM(a.shape, a.dtype) for a in operands] + [pltpu.SemaphoreType.DMA((9,))],
        compiler_params=params(60),
        name="projections",
    )(*operands)
    right = lax.all_to_all(right, ("y", "x"), 0, 0)
    other = lax.ppermute(left, "zu", SWAP)
    left = pl.pallas_call(
        join_kernel,
        out_shape=shape(2, 128, 128),
        compiler_params=params(16),
        cost_estimate=pl.CostEstimate(flops=10**10, bytes_accessed=0, transcendentals=0),
        name="join",
    )(left, other)
    for axis in ("zv", "zp"):
        left = lax.all_gather(left, axis, axis=0)
    left, right = lax.optimization_barrier((left, right))
    right_other = lax.ppermute(right, "core", SWAP)
    left = lax.all_gather(left, "core", axis=0).reshape(2, 8, 128, 128)

    parts, bias = pl.pallas_call(
        pair_kernel,
        out_shape=(shape(16, 16, 512), shape(1, 128, dtype=F32)),
        scratch_shapes=[
            pltpu.VMEM((1024, 128), F32),
            pltpu.VMEM((512, 256), BF16),
            pltpu.VMEM((256, 4096), BF16),
            pltpu.VMEM((4096, 512), BF16),
            pltpu.VMEM((1024, 128), F32),
        ],
        compiler_params=params(20),
        name="pair_block",
    )(left, right, right_other, mapping)
    parts = lax.all_to_all(parts, ("zh", "zu", "zv", "zp"), 0, 0)
    out = pl.pallas_call(
        final_kernel,
        out_shape=shape(512, 128),
        scratch_shapes=[pltpu.VMEM((512, 128), F32)],
        compiler_params=params(16),
        name="sum_and_bias",
    )(parts, bias)
    return out.reshape(1, 512, 128)


def solution(mesh):
    fine = Mesh(mesh.devices.reshape(4, 4, 2, 2, 2, 2, 2), AXES)
    placed = (P(("zh", "core"), ("y", "x", "zu", "zv", "zp"), None),) + (P(),) * 8
    return jax.shard_map(
        local, mesh=fine, in_specs=placed, out_specs=P(AXES, None, None), check_vma=False
    )
```

time: 70.5 us -> 68.3 us (0.969)
  blocking collectives: 53 us -> 43.6 us
  starting transfers between devices: 9.35 us -> 18.5 us
  Pallas kernels: 7.85 us -> 5.83 us
    ppermute x0 -> x2, starting transfers between devices: none -> 11 us  [the longest x1 9.1 us: local(): other = lax.ppermute(left, 'zu', SWAP)]
    all_gather x3 -> x2, blocking collectives: 20.2 us -> 12.3 us  [local(): left = lax.all_gather(left, axis, axis=0)]
    all_to_all x1, starting transfers between devices: 9.35 us -> 7.49 us  [local(): right = lax.all_to_all(right, ('y', 'x'), 0, 0)]
    all_to_all x1, blocking collectives: 30.7 us -> 29 us  [local(): parts = lax.all_to_all(parts, ('zh', 'zu', 'zv', 'zp'), 0, 0)]
    pallas_call x2, Pallas kernels: 4.2 us -> 2.73 us  [the longest x1 2.71 us: local(): pl.pallas_call(projection_kernel, out_shape=(shape(16, 128, 128), shape(1...]
  transfers between devices with their start and end apart: 1 -> 3, of which waited for: 0 -> 0; matrix products, arithmetic and copies ran while one was open for 0% -> 0% of each run, Pallas kernels for 0% -> 0%
where the time goes in v4:
time: 68.3 us; the launch traced here: 68 us
  blocking collectives  43.6 us (64%)
  starting transfers between devices  18.5 us (27%)
  Pallas kernels  5.83 us (9%)
    all_to_all x1, blocking collectives, local(): parts = lax.all_to_all(parts, ('zh', 'zu', 'zv', 'zp'), 0, 0)  29 us
    all_gather x2, blocking collectives, local(): left = lax.all_gather(left, axis, axis=0)  12.3 us
    ppermute x1, starting transfers between devices, local(): other = lax.ppermute(left, 'zu', SWAP)  9.1 us
    all_to_all x1, starting transfers between devices, local(): right = lax.all_to_all(right, ('y', 'x'), 0, 0)  7.49 us
    pallas_call x1, Pallas kernels, local(): pl.pallas_call(projection_kernel, out_shape=(shape(16, 128, 128), shape(1...  2.71 us
    all_gather x1, blocking collectives, local(): left = lax.all_gather(left, 'core', axis=0).reshape(2, 8, 128, 128)  2.31 us
    pallas_call x1, Pallas kernels, local(): pl.pallas_call(pair_kernel, out_shape=(shape(16, 16, 512), shape(1, 128,...  2.28 us
    ppermute x1, starting transfers between devices, local(): right_other = lax.ppermute(right, 'core', SWAP)  1.91 us
  transfers between devices with their start and end apart: 3, of which 0 were waited for; matrix products, arithmetic and copies ran while one was open for 0% of the time, Pallas kernels for 0%

profile of v4, /device:TPU:2, one launch (start us, length us, event | category | flops | bytes accessed | tf_op | source)
XLA Modules:
  0.0 68.0 jit_solution(400302653120173817)
XLA Ops:
  0.0 2.7 %projections.1 = (bf16[16,128,128]{2,1,0:T(8,128)(2,1)}, bf16[128,128]{1,0:T(8,128)(2,1)}, f32[1032,128]{1,0:T(8,128)}) custom-call(bf16[128,4,256]{2,1,0:T(4,128)(2,1)} %x_hbm.1, f32[1,256]{1,0:T(1,128)} %bitcast.16, f32[1,256]{1,0:T(1,128)} %bitcast.17, bf16[32,256]{1,0:T(8,128)(2,1)} %bitcast.14, f32[1,32]{1,0:T(1,128)} %bitcast.18, ...), custom_call_target="tpu_custom_call" | custom-call | tf_op jit(solution)/shard_map/projections/pallas_call | solution.py:126
  2.7 9.1 %collective-permute-start = (bf16[128,128]{1,0:T(8,128)(2,1)}, bf16[128,128]{1,0:T(8,128)(2,1)S(1)}, u32[]{:S(2)}, u32[]{:S(2)}) collective-permute-start(bf16[128,128]{1,0:T(8,128)(2,1)} %get-tuple-element.12.own_ref), channel_id=1, source_target_pairs={{0,16},{16,0},{1,17},{17,1},{2,18},{18,2},{3,19},{19,3},{4,20},{20... | collective-permute-start | bytes 98312 | tf_op jit(solution)/shard_map/ppermute | solution.py:135
  11.8 0.0 copy-start.1
  11.8 7.5 %all-to-all-start = ((bf16[16,128,128]{2,1,0:T(8,128)(2,1)}), bf16[16,128,128]{2,1,0:T(8,128)(2,1)S(1)}, u32[]{:S(2)}, u32[]{:S(2)}) async-start(bf16[16,128,128]{2,1,0:T(8,128)(2,1)} %get-tuple-element.13), calls=%async_computation | async-start | bytes 1048576 | tf_op jit(solution)/shard_map/all_to_all | solution.py:134
  19.3 0.0 collective-permute-done.other_ref
  19.3 0.0 copy-done.1
  19.4 6.5 %all-gather = bf16[4,128,128]{2,1,0:T(8,128)(2,1)S(1)} all-gather(bf16[2,128,128]{2,1,0:T(8,128)(2,1)S(1)} %join.1), channel_id=2, replica_groups=mesh['y'=4,'x'=4,'zu'=2,'zv'=2,'zp'=2,'zh'=2,'core'=2] {'zv'}, dimensions={0}, use_global_device_ids=true | all-gather | bytes 196608 | tf_op jit(solution)/shard_map/all_gather | solution.py:144
  25.9 0.0 copy-start
  25.9 5.8 %all-gather.1 = bf16[4,2,128,128]{3,2,1,0:T(8,128)(2,1)S(1)} all-gather(bf16[2,2,128,128]{3,2,1,0:T(8,128)(2,1)S(1)} %bitcast.13), channel_id=3, replica_groups=mesh['y'=4,'x'=4,'zu'=2,'zv'=2,'zp'=2,'zh'=2,'core'=2] {'zp'}, dimensions={0}, use_global_device_ids=true | all-gather | bytes 393216 | tf_op jit(solution)/shard_map/all_gather | solution.py:144
  31.7 0.0 all-to-all-done.right_ref
  31.7 1.9 %collective-permute-start.1 = (bf16[16,128,128]{2,1,0:T(8,128)(2,1)S(1)}, bf16[16,128,128]{2,1,0:T(8,128)(2,1)S(1)}, u32[]{:S(2)}, u32[]{:S(2)}) collective-permute-start(bf16[16,128,128]{2,1,0:T(8,128)(2,1)S(1)} %all-to-all-done.right_ref), channel_id=1, source_target_pairs={{0,1},{1,0},{2,3},{3,2},{4,5},{5,4},{6,7},{7,6},{8,9},{9,8},{10,11... | collective-permute-start | bytes 1572872 | tf_op jit(solution)/shard_map/ppermute | solution.py:146
  33.6 2.3 %all-gather.2 = bf16[4,2,2,128,128]{4,3,2,1,0:T(8,128)(2,1)S(1)} all-gather(bf16[2,2,2,128,128]{4,3,2,1,0:T(8,128)(2,1)S(1)} %bitcast.12), channel_id=4, replica_groups=mesh['y'=4,'x'=4,'zu'=2,'zv'=2,'zp'=2,'zh'=2,'core'=2] {'core'}, dimensions={0}, use_global_device_ids=true | all-gather | bytes 786432 | tf_op jit(solution)/shard_map/all_gather | solution.py:147
  35.9 0.0 collective-permute-done.1.other_ref
  35.9 0.0 copy-done
  35.9 2.3 %pair_block.1 = (bf16[16,16,512]{2,1,0:T(8,128)(2,1)S(1)}, f32[1,128]{1,0:T(1,128)S(1)}) custom-call(bf16[2,8,128,128]{3,2,1,0:T(8,128)(2,1)S(1)} %bitcast.11, bf16[16,128,128]{2,1,0:T(8,128)(2,1)S(1)} %all-to-all-done.right_ref, bf16[16,128,128]{2,1,0:T(8,128)(2,1)S(1)} %collective-permute-done.1.other_ref, f32[1032,128]{1,0:T(8,128)S(1)} %copy-done), custom_call_target="tpu_custom_call" | custom-call | tf_op jit(solution)/shard_map/pair_block/pallas_call | solution.py:149
  38.2 29.0 %all_to_all.10.parts_ref = bf16[16,16,512]{2,1,0:T(8,128)(2,1)S(1)} all-to-all(bf16[16,16,512]{2,1,0:T(8,128)(2,1)S(1)} %get-tuple-element.17), channel_id=1, replica_groups=mesh['y'=4,'x'=4,'zu'=2,'zv'=2,'zp'=2,'zh'=2,'core'=2] {'zh','zu','zv','..., dimensions={0} | all-to-all | bytes 524288 | tf_op jit(solution)/shard_map/all_to_all | solution.py:162
  67.1 0.8 %sum_and_bias.1 = bf16[512,128]{1,0:T(8,128)(2,1)} custom-call(bf16[16,16,512]{2,1,0:T(8,128)(2,1)S(1)} %all_to_all.10.parts_ref, f32[1,128]{1,0:T(1,128)S(1)} %get-tuple-element.18.bias_ref), custom_call_target="tpu_custom_call" | custom-call | tf_op jit(solution)/shard_map/sum_and_bias/pallas_call | solution.py:163
  (1 shorter events, 0.0 us)
Async XLA Ops:
  2.7 16.6 %collective-permute-start = (bf16[128,128]{1,0:T(8,128)(2,1)}, bf16[128,128]{1,0:T(8,128)(2,1)S(1)}, u32[]{:S(2)}, u32[]{:S(2)}) collective-permute-start(bf16[128,128]{1,0:T(8,128)(2,1)} %get-tuple-element.12.own_ref), channel_id=1, source_target_pairs={{0,16},{16,0},{1,17},{17,1},{2,18},{18,2},{3,19},{19,3},{4,20},{20... | collective-permute-start | bytes 98312 | tf_op jit(solution)/shard_map/ppermute | solution.py:135
  11.8 7.5 %copy-start.1 = (bf16[128,128]{1,0:T(8,128)(2,1)S(1)}, bf16[128,128]{1,0:T(8,128)(2,1)}, u32[]{:S(2)}) copy-start(bf16[128,128]{1,0:T(8,128)(2,1)} %get-tuple-element.12.own_ref) | copy-start | bytes 98308
  11.8 19.8 %all-to-all-start = ((bf16[16,128,128]{2,1,0:T(8,128)(2,1)}), bf16[16,128,128]{2,1,0:T(8,128)(2,1)S(1)}, u32[]{:S(2)}, u32[]{:S(2)}) async-start(bf16[16,128,128]{2,1,0:T(8,128)(2,1)} %get-tuple-element.13), calls=%async_computation | async-start | bytes 1048576 | tf_op jit(solution)/shard_map/all_to_all | solution.py:134
  25.9 10.0 %copy-start = (f32[1032,128]{1,0:T(8,128)S(1)}, f32[1032,128]{1,0:T(8,128)}, u32[]{:S(2)}) copy-start(f32[1032,128]{1,0:T(8,128)} %get-tuple-element.16.map_ref) | copy-start | bytes 1585156
  31.7 4.2 %collective-permute-start.1 = (bf16[16,128,128]{2,1,0:T(8,128)(2,1)S(1)}, bf16[16,128,128]{2,1,0:T(8,128)(2,1)S(1)}, u32[]{:S(2)}, u32[]{:S(2)}) collective-permute-start(bf16[16,128,128]{2,1,0:T(8,128)(2,1)S(1)} %all-to-all-done.right_ref), channel_id=1, source_target_pairs={{0,1},{1,0},{2,3},{3,2},{4,5},{5,4},{6,7},{7,6},{8,9},{9,8},{10,11... | collective-permute-start | bytes 1572872 | tf_op jit(solution)/shard_map/ppermute | solution.py:146

commit v5 on v4

--- a/solution.py
+++ b/solution.py
@@ -42,7 +42,7 @@
     rows = (rows + jnp.concatenate([bias] * 4, axis=1)).astype(BF16)
     rows = jnp.dot(rows, move, preferred_element_type=F32).astype(BF16)
     for r in range(4):
-        for to in range(16):
+        for to in range(32):
             right_out[to, r * 32 : r * 32 + 32, :] = rows[:32, r * 128 : r * 128 + 128]
         left_out[r * 32 : r * 32 + 32, :] = rows[32:, r * 128 : r * 128 + 128]
     for copy in copies[7:]:
@@ -57,17 +57,25 @@
     out_ref[1 - here] = other_ref[...]
 
 
-def pair_kernel(left_ref, right_ref, other_ref, map_ref, out_ref, bias_out, a32, a16, x16, wide_ref, res):
-    bias_out[...] = map_ref[1024:1025, :]
+def select_kernel(got_ref, out_ref):
     core = lax.axis_index("core")
-    for block, source in enumerate((core, 1 - core)):
-        for t in range(8):
-            zl = t % 2 * 4 + t // 2 % 2 * 2 + t // 4
+    for zu in range(2):
+        for block in range(2):
             for half in range(2):
                 row = pl.multiple_of((half * 2 + core) * 32, 32)
+                out_ref[zu, block, half * 32 : half * 32 + 32, :] = got_ref[block, zu, pl.ds(row, 32), :]
+
+
+def pair_kernel(left_ref, right_ref, map_ref, out_ref, bias_out, a32, a16, x16, wide_ref, res):
+    bias_out[...] = map_ref[1024:1025, :]
+    for t in range(8):
+        zl = t % 2 * 4 + t // 2 % 2 * 2 + t // 4
+        for block in range(2):
+            for half in range(2):
                 a32[pl.ds(block * 512 + zl * 2 + half, 32, stride=16), :] = left_ref[
-                    source, t, pl.ds(row, 32), :
+                    t, block, half * 32 : half * 32 + 32, :
                 ].astype(F32)
+    for block in range(2):
         a16[:, block * 128 : block * 128 + 128] = a32[block * 512 : block * 512 + 512, :].astype(BF16)
     wide_ref[...] = jnp.zeros_like(wide_ref)
     for c in range(32):
@@ -77,7 +85,7 @@
             ].astype(BF16)
     for first in range(0, 16, 4):
         chips = range(first, first + 4)
-        right = [jnp.concatenate([right_ref[yx], other_ref[yx]], axis=1) for yx in chips]
+        right = [jnp.concatenate([right_ref[yx % 4 * 8 + k * 4 + yx // 4] for k in range(2)], axis=1) for yx in chips]
         right = jnp.concatenate(right, axis=0)
         outer = lax.dot_general(a16[...], right, NT, preferred_element_type=F32).astype(BF16)
         for k, yx in enumerate(chips):
@@ -123,15 +131,16 @@
         second_bias.reshape(1, 32),
     )
     operands += (mapping, final_bias.reshape(1, 128))
+    operands = tuple(pltpu.with_memory_space_constraint(a, pltpu.HBM) for a in operands)
     right, left, mapping = pl.pallas_call(
         projection_kernel,
-        out_shape=(shape(16, 128, 128), shape(128, 128), shape(1032, 128, dtype=F32)),
+        out_shape=(shape(32, 128, 128), shape(128, 128), shape(1032, 128, dtype=F32)),
         in_specs=[pl.BlockSpec(memory_space=pltpu.HBM)] * 9,
         scratch_shapes=[pltpu.VMEM(a.shape, a.dtype) for a in operands] + [pltpu.SemaphoreType.DMA((9,))],
-        compiler_params=params(60),
+        compiler_params=params(16),
         name="projections",
     )(*operands)
-    right = lax.all_to_all(right, ("y", "x"), 0, 0)
+    right = lax.all_to_all(right, ("x", "core", "y"), 0, 0)
     other = lax.ppermute(left, "zu", SWAP)
     left = pl.pallas_call(
         join_kernel,
@@ -140,11 +149,16 @@
         cost_estimate=pl.CostEstimate(flops=10**10, bytes_accessed=0, transcendentals=0),
         name="join",
     )(left, other)
+    left = lax.all_gather(left, "core", axis=0)
+    left = pl.pallas_call(
+        select_kernel,
+        out_shape=shape(2, 2, 64, 128),
+        compiler_params=params(16),
+        name="select",
+    )(left)
     for axis in ("zv", "zp"):
         left = lax.all_gather(left, axis, axis=0)
-    left, right = lax.optimization_barrier((left, right))
-    right_other = lax.ppermute(right, "core", SWAP)
-    left = lax.all_gather(left, "core", axis=0).reshape(2, 8, 128, 128)
+    left = left.reshape(8, 2, 64, 128)
 
     parts, bias = pl.pallas_call(
         pair_kernel,
@@ -158,7 +172,7 @@
         ],
         compiler_params=params(20),
         name="pair_block",
-    )(left, right, right_other, mapping)
+    )(left, right, mapping)
     parts = lax.all_to_all(parts, ("zh", "zu", "zv", "zp"), 0, 0)
     out = pl.pallas_call(
         final_kernel,

time: 68.3 us -> 67.9 us (level)
  the two profiles are of different devices: /device:TPU:2 before, /device:TPU:64 now
where the time goes in v5:
time: 67.9 us; the launch traced here: 67.6 us
  blocking collectives  43.1 us (63%)
  starting transfers between devices  16.4 us (24%)
  Pallas kernels  5.9 us (9%)
  waiting for transfers between devices  2.13 us (3%)
    all_to_all x1, blocking collectives, local(): parts = lax.all_to_all(parts, ('zh', 'zu', 'zv', 'zp'), 0, 0)  28.1 us
    all_gather x2, blocking collectives, local(): left = lax.all_gather(left, axis, axis=0)  13.1 us
    ppermute x1, starting transfers between devices, local(): other = lax.ppermute(left, 'zu', SWAP)  9.1 us
    all_to_all x1, starting transfers between devices, local(): right = lax.all_to_all(right, ('x', 'core', 'y'), 0, 0)  7.33 us
    pallas_call x1, Pallas kernels, local(): pl.pallas_call(projection_kernel, out_shape=(shape(32, 128, 128), shape(1...  2.77 us
    pallas_call x1, Pallas kernels, local(): pl.pallas_call(pair_kernel, out_shape=(shape(16, 16, 512), shape(1, 128,...  2.28 us
    all_to_all x1, waiting for transfers between devices, local(): right = lax.all_to_all(right, ('x', 'core', 'y'), 0, 0)  2.12 us
    all_gather x1, blocking collectives, local(): left = lax.all_gather(left, 'core', axis=0)  1.9 us
  transfers between devices with their start and end apart: 2, of which 1 were waited for; matrix products, arithmetic and copies ran while one was open for 0% of the time, Pallas kernels for 0%

profile of v5, /device:TPU:64, one launch (start us, length us, event | category | flops | bytes accessed | tf_op | source)
XLA Modules:
  0.0 67.6 jit_solution(15177528635027518598)
XLA Ops:
  0.0 2.8 %projections.1 = (bf16[32,128,128]{2,1,0:T(8,128)(2,1)}, bf16[128,128]{1,0:T(8,128)(2,1)S(1)}, f32[1032,128]{1,0:T(8,128)S(1)}) custom-call(bf16[128,4,256]{2,1,0:T(4,128)(2,1)} %x_hbm.1, f32[1,256]{1,0:T(1,128)} %bitcast.16, f32[1,256]{1,0:T(1,128)} %bitcast.17, bf16[32,256]{1,0:T(8,128)(2,1)} %bitcast.14, f32[1,32]{1,0:T(1,128)} %bitcast.18, ...), custom_call_target="tpu_custom_call" | custom-call | tf_op jit(solution)/shard_map/projections/pallas_call | solution.py:135
  2.8 9.1 %collective-permute-start = (bf16[128,128]{1,0:T(8,128)(2,1)S(1)}, bf16[128,128]{1,0:T(8,128)(2,1)S(1)}, u32[]{:S(2)}, u32[]{:S(2)}) collective-permute-start(bf16[128,128]{1,0:T(8,128)(2,1)S(1)} %get-tuple-element.10.own_ref), channel_id=1, source_target_pairs={{0,16},{16,0},{1,17},{17,1},{2,18},{18,2},{3,19},{19,3},{4,20},{20... | collective-permute-start | bytes 98312 | tf_op jit(solution)/shard_map/ppermute | solution.py:144
  11.9 7.3 %all-to-all-start = ((bf16[32,128,128]{2,1,0:T(8,128)(2,1)}), bf16[32,128,128]{2,1,0:T(8,128)(2,1)S(1)}, u32[]{:S(2)}, u32[]{:S(2)}) async-start(bf16[32,128,128]{2,1,0:T(8,128)(2,1)} %get-tuple-element.11), calls=%async_computation | async-start | bytes 2097152 | tf_op jit(solution)/shard_map/all_to_all | solution.py:143
  19.2 0.0 collective-permute-done.other_ref
  19.3 1.9 %all-gather = bf16[4,128,128]{2,1,0:T(8,128)(2,1)S(1)} all-gather(bf16[2,128,128]{2,1,0:T(8,128)(2,1)S(1)} %join.1), channel_id=2, replica_groups=mesh['y'=4,'x'=4,'zu'=2,'zv'=2,'zp'=2,'zh'=2,'core'=2] {'core'}, dimensions={0}, use_global_device_ids=true | all-gather | bytes 196608 | tf_op jit(solution)/shard_map/all_gather | solution.py:152
  21.2 5.9 %all-gather.1 = bf16[4,2,64,128]{3,2,1,0:T(8,128)(2,1)S(1)} all-gather(bf16[2,2,64,128]{3,2,1,0:T(8,128)(2,1)S(1)} %select.1), channel_id=3, replica_groups=mesh['y'=4,'x'=4,'zu'=2,'zv'=2,'zp'=2,'zh'=2,'core'=2] {'zv'}, dimensions={0}, use_global_device_ids=true | all-gather | bytes 196608 | tf_op jit(solution)/shard_map/all_gather | solution.py:160
  27.1 7.1 %all-gather.2 = bf16[4,2,2,64,128]{4,3,2,1,0:T(8,128)(2,1)S(1)} all-gather(bf16[2,2,2,64,128]{4,3,2,1,0:T(8,128)(2,1)S(1)} %bitcast.13), channel_id=4, replica_groups=mesh['y'=4,'x'=4,'zu'=2,'zv'=2,'zp'=2,'zh'=2,'core'=2] {'zp'}, dimensions={0}, use_global_device_ids=true | all-gather | bytes 393216 | tf_op jit(solution)/shard_map/all_gather | solution.py:160
  34.2 2.1 %all-to-all-done.right_ref = bf16[32,128,128]{2,1,0:T(8,128)(2,1)S(1)} async-done(((bf16[32,128,128]{2,1,0:T(8,128)(2,1)}), bf16[32,128,128]{2,1,0:T(8,128)(2,1)S(1)}, u32[]{:S(2)}, u32[]{:S(2)}) %all-to-all-start) | async-done | bytes 1048608 | tf_op jit(solution)/shard_map/all_to_all | solution.py:143
  36.3 2.3 %pair_block.1 = (bf16[16,16,512]{2,1,0:T(8,128)(2,1)S(1)}, f32[1,128]{1,0:T(1,128)S(1)}) custom-call(bf16[8,2,64,128]{3,2,1,0:T(8,128)(2,1)S(1)} %bitcast.11, bf16[32,128,128]{2,1,0:T(8,128)(2,1)S(1)} %all-to-all-done.right_ref, f32[1032,128]{1,0:T(8,128)S(1)} %get-tuple-element.12.map_ref), custom_call_target="tpu_custom_call" | custom-call | tf_op jit(solution)/shard_map/pair_block/pallas_call | solution.py:163
  38.6 28.1 %all_to_all.10.parts_ref = bf16[16,16,512]{2,1,0:T(8,128)(2,1)S(1)} all-to-all(bf16[16,16,512]{2,1,0:T(8,128)(2,1)S(1)} %get-tuple-element.13), channel_id=1, replica_groups=mesh['y'=4,'x'=4,'zu'=2,'zv'=2,'zp'=2,'zh'=2,'core'=2] {'zh','zu','zv','..., dimensions={0} | all-to-all | bytes 524288 | tf_op jit(solution)/shard_map/all_to_all | solution.py:176
  66.8 0.8 %sum_and_bias.1 = bf16[512,128]{1,0:T(8,128)(2,1)} custom-call(bf16[16,16,512]{2,1,0:T(8,128)(2,1)S(1)} %all_to_all.10.parts_ref, f32[1,128]{1,0:T(1,128)S(1)} %get-tuple-element.14.bias_ref), custom_call_target="tpu_custom_call" | custom-call | tf_op jit(solution)/shard_map/sum_and_bias/pallas_call | solution.py:177
  (2 shorter events, 0.0 us)
Async XLA Ops:
  2.8 16.4 %collective-permute-start = (bf16[128,128]{1,0:T(8,128)(2,1)S(1)}, bf16[128,128]{1,0:T(8,128)(2,1)S(1)}, u32[]{:S(2)}, u32[]{:S(2)}) collective-permute-start(bf16[128,128]{1,0:T(8,128)(2,1)S(1)} %get-tuple-element.10.own_ref), channel_id=1, source_target_pairs={{0,16},{16,0},{1,17},{17,1},{2,18},{18,2},{3,19},{19,3},{4,20},{20... | collective-permute-start | bytes 98312 | tf_op jit(solution)/shard_map/ppermute | solution.py:144
  11.9 24.5 %all-to-all-start = ((bf16[32,128,128]{2,1,0:T(8,128)(2,1)}), bf16[32,128,128]{2,1,0:T(8,128)(2,1)S(1)}, u32[]{:S(2)}, u32[]{:S(2)}) async-start(bf16[32,128,128]{2,1,0:T(8,128)(2,1)} %get-tuple-element.11), calls=%async_computation | async-start | bytes 2097152 | tf_op jit(solution)/shard_map/all_to_all | solution.py:143

commit v6 on v5

--- a/solution.py
+++ b/solution.py
@@ -8,17 +8,18 @@
 F32 = jnp.float32
 BF16 = jnp.bfloat16
 AXES = ("y", "x", "zu", "zv", "zp", "zh", "core")
+RING = ("zp", "zh", "zv", "zu")
 SWAP = [(0, 1), (1, 0)]
 NT = (((1,), (1,)), ((), ()))
 
 
 def projection_kernel(
     x_hbm, gain_hbm, offset_hbm, left_hbm, left_bias_hbm, right_hbm, right_bias_hbm, map_hbm, bias_hbm,
-    right_out, left_out, map_out,
-    x_ref, gain_ref, offset_ref, left_ref, left_bias_ref, right_ref, right_bias_ref, map_ref, bias_ref, sems,
+    right_out, left_out, map_out, bias_out,
+    x_ref, gain_ref, offset_ref, left_ref, left_bias_ref, right_ref, right_bias_ref, sems,
 ):
     sources = (x_hbm, gain_hbm, offset_hbm, left_hbm, left_bias_hbm, right_hbm, right_bias_hbm, map_hbm, bias_hbm)
-    targets = (x_ref, gain_ref, offset_ref, left_ref, left_bias_ref, right_ref, right_bias_ref, map_ref, bias_ref)
+    targets = (x_ref, gain_ref, offset_ref, left_ref, left_bias_ref, right_ref, right_bias_ref, map_out, bias_out)
     copies = [
         pltpu.make_async_copy(src, dst, sems.at[k]) for k, (src, dst) in enumerate(zip(sources, targets))
     ]
@@ -47,8 +48,6 @@
         left_out[r * 32 : r * 32 + 32, :] = rows[32:, r * 128 : r * 128 + 128]
     for copy in copies[7:]:
         copy.wait()
-    map_out[:1024, :] = map_ref[...].astype(F32)
-    map_out[1024:, :] = jnp.broadcast_to(bias_ref[...], (8, 128))
 
 
 def join_kernel(own_ref, other_ref, out_ref):
@@ -66,8 +65,7 @@
                 out_ref[zu, block, half * 32 : half * 32 + 32, :] = got_ref[block, zu, pl.ds(row, 32), :]
 
 
-def pair_kernel(left_ref, right_ref, map_ref, out_ref, bias_out, a32, a16, x16, wide_ref, res):
-    bias_out[...] = map_ref[1024:1025, :]
+def pair_kernel(left_ref, right_ref, map_ref, out_ref, a32, a16, x16, wide_ref, res):
     for t in range(8):
         zl = t % 2 * 4 + t // 2 % 2 * 2 + t // 4
         for block in range(2):
@@ -82,7 +80,7 @@
         for r in range(4):
             wide_ref[c * 128 + r * 32 : c * 128 + r * 32 + 32, r * 128 : r * 128 + 128] = map_ref[
                 c * 32 : c * 32 + 32, :
-            ].astype(BF16)
+            ]
     for first in range(0, 16, 4):
         chips = range(first, first + 4)
         right = [jnp.concatenate([right_ref[yx % 4 * 8 + k * 4 + yx // 4] for k in range(2)], axis=1) for yx in chips]
@@ -98,15 +96,19 @@
         res[r * 256 : r * 256 + 256, :] = total[:, r * 128 : r * 128 + 128]
     for k in range(8):
         for half in range(2):
-            to = half * 8 + k
+            to = ring_rank(k, half)
             for r in range(4):
                 rows = res[pl.ds(r * 256 + k * 2 + half, 16, stride=16), :]
                 out_ref[to, :, r * 128 : r * 128 + 128] = rows.astype(BF16)
 
 
+def ring_rank(zl, half):
+    return zl % 2 * 8 + half * 4 + zl // 2 % 2 * 2 + zl // 4
+
+
 def final_kernel(parts_ref, bias_ref, out_ref, rows):
     for zl in range(8):
-        summed = parts_ref[zl].astype(F32) + parts_ref[8 + zl].astype(F32)
+        summed = parts_ref[ring_rank(zl, 0)].astype(F32) + parts_ref[ring_rank(zl, 1)].astype(F32)
         for r in range(4):
             rows[pl.ds(zl * 4 + r, 16, stride=32), :] = summed[:, r * 128 : r * 128 + 128] + bias_ref[...]
     out_ref[...] = rows[...].astype(BF16)
@@ -132,11 +134,11 @@
     )
     operands += (mapping, final_bias.reshape(1, 128))
     operands = tuple(pltpu.with_memory_space_constraint(a, pltpu.HBM) for a in operands)
-    right, left, mapping = pl.pallas_call(
+    right, left, mapping, bias = pl.pallas_call(
         projection_kernel,
-        out_shape=(shape(32, 128, 128), shape(128, 128), shape(1032, 128, dtype=F32)),
+        out_shape=(shape(32, 128, 128), shape(128, 128), shape(1024, 128), shape(1, 128, dtype=F32)),
         in_specs=[pl.BlockSpec(memory_space=pltpu.HBM)] * 9,
-        scratch_shapes=[pltpu.VMEM(a.shape, a.dtype) for a in operands] + [pltpu.SemaphoreType.DMA((9,))],
+        scratch_shapes=[pltpu.VMEM(a.shape, a.dtype) for a in operands[:7]] + [pltpu.SemaphoreType.DMA((9,))],
         compiler_params=params(16),
         name="projections",
     )(*operands)
@@ -160,9 +162,9 @@
         left = lax.all_gather(left, axis, axis=0)
     left = left.reshape(8, 2, 64, 128)
 
-    parts, bias = pl.pallas_call(
+    parts = pl.pallas_call(
         pair_kernel,
-        out_shape=(shape(16, 16, 512), shape(1, 128, dtype=F32)),
+        out_shape=shape(16, 16, 512),
         scratch_shapes=[
             pltpu.VMEM((1024, 128), F32),
             pltpu.VMEM((512, 256), BF16),
@@ -173,7 +175,7 @@
         compiler_params=params(20),
         name="pair_block",
     )(left, right, mapping)
-    parts = lax.all_to_all(parts, ("zh", "zu", "zv", "zp"), 0, 0)
+    parts = lax.all_to_all(parts, RING, 0, 0)
     out = pl.pallas_call(
         final_kernel,
         out_shape=shape(512, 128),

time: 67.9 us -> 67.7 us (level)
  the two profiles are of different devices: /device:TPU:64 before, /device:TPU:32 now
where the time goes in v6:
time: 67.7 us; the launch traced here: 67.4 us
  blocking collectives  42.7 us (63%)
  starting transfers between devices  16.4 us (24%)
  Pallas kernels  5.88 us (9%)
  waiting for transfers between devices  2.39 us (4%)
    all_to_all x1, blocking collectives, local(): parts = lax.all_to_all(parts, RING, 0, 0)  28 us
    all_gather x2, blocking collectives, local(): left = lax.all_gather(left, axis, axis=0)  12.8 us
    ppermute x1, starting transfers between devices, local(): other = lax.ppermute(left, 'zu', SWAP)  9.1 us
    all_to_all x1, starting transfers between devices, local(): right = lax.all_to_all(right, ('x', 'core', 'y'), 0, 0)  7.33 us
    pallas_call x1, Pallas kernels, local(): pl.pallas_call(projection_kernel, out_shape=(shape(32, 128, 128), shape(1...  2.77 us
    all_to_all x1, waiting for transfers between devices, local(): right = lax.all_to_all(right, ('x', 'core', 'y'), 0, 0)  2.39 us
    pallas_call x1, Pallas kernels, local(): pl.pallas_call(pair_kernel, out_shape=shape(16, 16, 512), scratch_shapes=...  2.27 us
    all_gather x1, blocking collectives, local(): left = lax.all_gather(left, 'core', axis=0)  1.9 us
  transfers between devices with their start and end apart: 2, of which 1 were waited for; matrix products, arithmetic and copies ran while one was open for 0% of the time, Pallas kernels for 0%

profile of v6, /device:TPU:32, one launch (start us, length us, event | category | flops | bytes accessed | tf_op | source)
XLA Modules:
  0.0 67.4 jit_solution(10901206707138076486)
XLA Ops:
  0.0 2.8 %projections.1 = (bf16[32,128,128]{2,1,0:T(8,128)(2,1)}, bf16[128,128]{1,0:T(8,128)(2,1)S(1)}, bf16[1024,128]{1,0:T(8,128)(2,1)S(1)}, f32[1,128]{1,0:T(1,128)S(1)}) custom-call(bf16[128,4,256]{2,1,0:T(4,128)(2,1)} %x_hbm.1, f32[1,256]{1,0:T(1,128)} %bitcast.16, f32[1,256]{1,0:T(1,128)} %bitcast.17, bf16[32,256]{1,0:T(8,128)(2,1)} %bitcast.14, ...), custom_call_target="tpu_custom_call" | custom-call | tf_op jit(solution)/shard_map/projections/pallas_call | solution.py:137
  2.8 9.1 %collective-permute-start = (bf16[128,128]{1,0:T(8,128)(2,1)S(1)}, bf16[128,128]{1,0:T(8,128)(2,1)S(1)}, u32[]{:S(2)}, u32[]{:S(2)}) collective-permute-start(bf16[128,128]{1,0:T(8,128)(2,1)S(1)} %get-tuple-element.9.own_ref), channel_id=1, source_target_pairs={{0,16},{16,0},{1,17},{17,1},{2,18},{18,2},{3,19},{19,3},{4,20},{20... | collective-permute-start | bytes 98312 | tf_op jit(solution)/shard_map/ppermute | solution.py:146
  11.9 7.3 %all-to-all-start = ((bf16[32,128,128]{2,1,0:T(8,128)(2,1)}), bf16[32,128,128]{2,1,0:T(8,128)(2,1)S(1)}, u32[]{:S(2)}, u32[]{:S(2)}) async-start(bf16[32,128,128]{2,1,0:T(8,128)(2,1)} %get-tuple-element.10), calls=%async_computation | async-start | bytes 2097152 | tf_op jit(solution)/shard_map/all_to_all | solution.py:145
  19.2 0.0 collective-permute-done.other_ref
  19.3 1.9 %all-gather = bf16[4,128,128]{2,1,0:T(8,128)(2,1)S(1)} all-gather(bf16[2,128,128]{2,1,0:T(8,128)(2,1)S(1)} %join.1), channel_id=2, replica_groups=mesh['y'=4,'x'=4,'zu'=2,'zv'=2,'zp'=2,'zh'=2,'core'=2] {'core'}, dimensions={0}, use_global_device_ids=true | all-gather | bytes 196608 | tf_op jit(solution)/shard_map/all_gather | solution.py:154
  21.2 6.7 %all-gather.1 = bf16[4,2,64,128]{3,2,1,0:T(8,128)(2,1)S(1)} all-gather(bf16[2,2,64,128]{3,2,1,0:T(8,128)(2,1)S(1)} %select.1), channel_id=3, replica_groups=mesh['y'=4,'x'=4,'zu'=2,'zv'=2,'zp'=2,'zh'=2,'core'=2] {'zv'}, dimensions={0}, use_global_device_ids=true | all-gather | bytes 196608 | tf_op jit(solution)/shard_map/all_gather | solution.py:162
  27.9 6.1 %all-gather.2 = bf16[4,2,2,64,128]{4,3,2,1,0:T(8,128)(2,1)S(1)} all-gather(bf16[2,2,2,64,128]{4,3,2,1,0:T(8,128)(2,1)S(1)} %bitcast.13), channel_id=4, replica_groups=mesh['y'=4,'x'=4,'zu'=2,'zv'=2,'zp'=2,'zh'=2,'core'=2] {'zp'}, dimensions={0}, use_global_device_ids=true | all-gather | bytes 393216 | tf_op jit(solution)/shard_map/all_gather | solution.py:162
  34.0 2.4 %all-to-all-done.right_ref = bf16[32,128,128]{2,1,0:T(8,128)(2,1)S(1)} async-done(((bf16[32,128,128]{2,1,0:T(8,128)(2,1)}), bf16[32,128,128]{2,1,0:T(8,128)(2,1)S(1)}, u32[]{:S(2)}, u32[]{:S(2)}) %all-to-all-start) | async-done | bytes 1048608 | tf_op jit(solution)/shard_map/all_to_all | solution.py:145
  36.4 2.3 %pair_block.1 = bf16[16,16,512]{2,1,0:T(8,128)(2,1)S(1)} custom-call(bf16[8,2,64,128]{3,2,1,0:T(8,128)(2,1)S(1)} %bitcast.11, bf16[32,128,128]{2,1,0:T(8,128)(2,1)S(1)} %all-to-all-done.right_ref, bf16[1024,128]{1,0:T(8,128)(2,1)S(1)} %get-tuple-element.11.map_ref), custom_call_target="tpu_custom_call" | custom-call | tf_op jit(solution)/shard_map/pair_block/pallas_call | solution.py:165
  38.6 28.0 %all_to_all.10.parts_ref = bf16[16,16,512]{2,1,0:T(8,128)(2,1)S(1)} all-to-all(bf16[16,16,512]{2,1,0:T(8,128)(2,1)S(1)} %pair_block.1), channel_id=1, replica_groups=mesh['y'=4,'x'=4,'zu'=2,'zv'=2,'zp'=2,'zh'=2,'core'=2] {'zp','zh','zv','..., dimensions={0} | all-to-all | bytes 524288 | tf_op jit(solution)/shard_map/all_to_all | solution.py:178
  66.6 0.8 %sum_and_bias.1 = bf16[512,128]{1,0:T(8,128)(2,1)} custom-call(bf16[16,16,512]{2,1,0:T(8,128)(2,1)S(1)} %all_to_all.10.parts_ref, f32[1,128]{1,0:T(1,128)S(1)} %get-tuple-element.12.bias_ref), custom_call_target="tpu_custom_call" | custom-call | tf_op jit(solution)/shard_map/sum_and_bias/pallas_call | solution.py:179
  (2 shorter events, 0.0 us)
Async XLA Ops:
  2.8 16.4 %collective-permute-start = (bf16[128,128]{1,0:T(8,128)(2,1)S(1)}, bf16[128,128]{1,0:T(8,128)(2,1)S(1)}, u32[]{:S(2)}, u32[]{:S(2)}) collective-permute-start(bf16[128,128]{1,0:T(8,128)(2,1)S(1)} %get-tuple-element.9.own_ref), channel_id=1, source_target_pairs={{0,16},{16,0},{1,17},{17,1},{2,18},{18,2},{3,19},{19,3},{4,20},{20... | collective-permute-start | bytes 98312 | tf_op jit(solution)/shard_map/ppermute | solution.py:146
  11.9 24.5 %all-to-all-start = ((bf16[32,128,128]{2,1,0:T(8,128)(2,1)}), bf16[32,128,128]{2,1,0:T(8,128)(2,1)S(1)}, u32[]{:S(2)}, u32[]{:S(2)}) async-start(bf16[32,128,128]{2,1,0:T(8,128)(2,1)} %get-tuple-element.10), calls=%async_computation | async-start | bytes 2097152 | tf_op jit(solution)/shard_map/all_to_all | solution.py:145

commit v7 on v6

--- a/solution.py
+++ b/solution.py
@@ -131,8 +131,9 @@
         first_bias.reshape(1, 32),
         second.T,
         second_bias.reshape(1, 32),
+        mapping,
+        final_bias.reshape(1, 128),
     )
-    operands += (mapping, final_bias.reshape(1, 128))
     operands = tuple(pltpu.with_memory_space_constraint(a, pltpu.HBM) for a in operands)
     right, left, mapping, bias = pl.pallas_call(
         projection_kernel,

time: 67.7 us -> 67.7 us (level)
  no operation moved by 1% of the time
where the time goes in v7:
time: 67.7 us; the launch traced here: 67.4 us
  blocking collectives  42.7 us (63%)
  starting transfers between devices  16.4 us (24%)
  Pallas kernels  5.88 us (9%)
  waiting for transfers between devices  2.39 us (4%)
    all_to_all x1, blocking collectives, local(): parts = lax.all_to_all(parts, RING, 0, 0)  28 us
    all_gather x2, blocking collectives, local(): left = lax.all_gather(left, axis, axis=0)  12.8 us
    ppermute x1, starting transfers between devices, local(): other = lax.ppermute(left, 'zu', SWAP)  9.1 us
    all_to_all x1, starting transfers between devices, local(): right = lax.all_to_all(right, ('x', 'core', 'y'), 0, 0)  7.33 us
    pallas_call x1, Pallas kernels, local(): pl.pallas_call(projection_kernel, out_shape=(shape(32, 128, 128), shape(1...  2.77 us
    all_to_all x1, waiting for transfers between devices, local(): right = lax.all_to_all(right, ('x', 'core', 'y'), 0, 0)  2.39 us
    pallas_call x1, Pallas kernels, local(): pl.pallas_call(pair_kernel, out_shape=shape(16, 16, 512), scratch_shapes=...  2.27 us
    all_gather x1, blocking collectives, local(): left = lax.all_gather(left, 'core', axis=0)  1.9 us
  transfers between devices with their start and end apart: 2, of which 1 were waited for; matrix products, arithmetic and copies ran while one was open for 0% of the time, Pallas kernels for 0%

profile of v7, /device:TPU:32, one launch (start us, length us, event | category | flops | bytes accessed | tf_op | source)
XLA Modules:
  0.0 67.4 jit_solution(10901206707138076486)
XLA Ops:
  0.0 2.8 %projections.1 = (bf16[32,128,128]{2,1,0:T(8,128)(2,1)}, bf16[128,128]{1,0:T(8,128)(2,1)S(1)}, bf16[1024,128]{1,0:T(8,128)(2,1)S(1)}, f32[1,128]{1,0:T(1,128)S(1)}) custom-call(bf16[128,4,256]{2,1,0:T(4,128)(2,1)} %x_hbm.1, f32[1,256]{1,0:T(1,128)} %bitcast.16, f32[1,256]{1,0:T(1,128)} %bitcast.17, bf16[32,256]{1,0:T(8,128)(2,1)} %bitcast.14, ...), custom_call_target="tpu_custom_call" | custom-call | tf_op jit(solution)/shard_map/projections/pallas_call | solution.py:138
  2.8 9.1 %collective-permute-start = (bf16[128,128]{1,0:T(8,128)(2,1)S(1)}, bf16[128,128]{1,0:T(8,128)(2,1)S(1)}, u32[]{:S(2)}, u32[]{:S(2)}) collective-permute-start(bf16[128,128]{1,0:T(8,128)(2,1)S(1)} %get-tuple-element.9.own_ref), channel_id=1, source_target_pairs={{0,16},{16,0},{1,17},{17,1},{2,18},{18,2},{3,19},{19,3},{4,20},{20... | collective-permute-start | bytes 98312 | tf_op jit(solution)/shard_map/ppermute | solution.py:147
  11.9 7.3 %all-to-all-start = ((bf16[32,128,128]{2,1,0:T(8,128)(2,1)}), bf16[32,128,128]{2,1,0:T(8,128)(2,1)S(1)}, u32[]{:S(2)}, u32[]{:S(2)}) async-start(bf16[32,128,128]{2,1,0:T(8,128)(2,1)} %get-tuple-element.10), calls=%async_computation | async-start | bytes 2097152 | tf_op jit(solution)/shard_map/all_to_all | solution.py:146
  19.2 0.0 collective-permute-done.other_ref
  19.3 1.9 %all-gather = bf16[4,128,128]{2,1,0:T(8,128)(2,1)S(1)} all-gather(bf16[2,128,128]{2,1,0:T(8,128)(2,1)S(1)} %join.1), channel_id=2, replica_groups=mesh['y'=4,'x'=4,'zu'=2,'zv'=2,'zp'=2,'zh'=2,'core'=2] {'core'}, dimensions={0}, use_global_device_ids=true | all-gather | bytes 196608 | tf_op jit(solution)/shard_map/all_gather | solution.py:155
  21.2 6.7 %all-gather.1 = bf16[4,2,64,128]{3,2,1,0:T(8,128)(2,1)S(1)} all-gather(bf16[2,2,64,128]{3,2,1,0:T(8,128)(2,1)S(1)} %select.1), channel_id=3, replica_groups=mesh['y'=4,'x'=4,'zu'=2,'zv'=2,'zp'=2,'zh'=2,'core'=2] {'zv'}, dimensions={0}, use_global_device_ids=true | all-gather | bytes 196608 | tf_op jit(solution)/shard_map/all_gather | solution.py:163
  27.9 6.1 %all-gather.2 = bf16[4,2,2,64,128]{4,3,2,1,0:T(8,128)(2,1)S(1)} all-gather(bf16[2,2,2,64,128]{4,3,2,1,0:T(8,128)(2,1)S(1)} %bitcast.13), channel_id=4, replica_groups=mesh['y'=4,'x'=4,'zu'=2,'zv'=2,'zp'=2,'zh'=2,'core'=2] {'zp'}, dimensions={0}, use_global_device_ids=true | all-gather | bytes 393216 | tf_op jit(solution)/shard_map/all_gather | solution.py:163
  34.0 2.4 %all-to-all-done.right_ref = bf16[32,128,128]{2,1,0:T(8,128)(2,1)S(1)} async-done(((bf16[32,128,128]{2,1,0:T(8,128)(2,1)}), bf16[32,128,128]{2,1,0:T(8,128)(2,1)S(1)}, u32[]{:S(2)}, u32[]{:S(2)}) %all-to-all-start) | async-done | bytes 1048608 | tf_op jit(solution)/shard_map/all_to_all | solution.py:146
  36.4 2.3 %pair_block.1 = bf16[16,16,512]{2,1,0:T(8,128)(2,1)S(1)} custom-call(bf16[8,2,64,128]{3,2,1,0:T(8,128)(2,1)S(1)} %bitcast.11, bf16[32,128,128]{2,1,0:T(8,128)(2,1)S(1)} %all-to-all-done.right_ref, bf16[1024,128]{1,0:T(8,128)(2,1)S(1)} %get-tuple-element.11.map_ref), custom_call_target="tpu_custom_call" | custom-call | tf_op jit(solution)/shard_map/pair_block/pallas_call | solution.py:166
  38.6 28.0 %all_to_all.10.parts_ref = bf16[16,16,512]{2,1,0:T(8,128)(2,1)S(1)} all-to-all(bf16[16,16,512]{2,1,0:T(8,128)(2,1)S(1)} %pair_block.1), channel_id=1, replica_groups=mesh['y'=4,'x'=4,'zu'=2,'zv'=2,'zp'=2,'zh'=2,'core'=2] {'zp','zh','zv','..., dimensions={0} | all-to-all | bytes 524288 | tf_op jit(solution)/shard_map/all_to_all | solution.py:179
  66.6 0.8 %sum_and_bias.1 = bf16[512,128]{1,0:T(8,128)(2,1)} custom-call(bf16[16,16,512]{2,1,0:T(8,128)(2,1)S(1)} %all_to_all.10.parts_ref, f32[1,128]{1,0:T(1,128)S(1)} %get-tuple-element.12.bias_ref), custom_call_target="tpu_custom_call" | custom-call | tf_op jit(solution)/shard_map/sum_and_bias/pallas_call | solution.py:180
  (2 shorter events, 0.0 us)
Async XLA Ops:
  2.8 16.4 %collective-permute-start = (bf16[128,128]{1,0:T(8,128)(2,1)S(1)}, bf16[128,128]{1,0:T(8,128)(2,1)S(1)}, u32[]{:S(2)}, u32[]{:S(2)}) collective-permute-start(bf16[128,128]{1,0:T(8,128)(2,1)S(1)} %get-tuple-element.9.own_ref), channel_id=1, source_target_pairs={{0,16},{16,0},{1,17},{17,1},{2,18},{18,2},{3,19},{19,3},{4,20},{20... | collective-permute-start | bytes 98312 | tf_op jit(solution)/shard_map/ppermute | solution.py:147
  11.9 24.5 %all-to-all-start = ((bf16[32,128,128]{2,1,0:T(8,128)(2,1)}), bf16[32,128,128]{2,1,0:T(8,128)(2,1)S(1)}, u32[]{:S(2)}, u32[]{:S(2)}) async-start(bf16[32,128,128]{2,1,0:T(8,128)(2,1)} %get-tuple-element.10), calls=%async_computation | async-start | bytes 2097152 | tf_op jit(solution)/shard_map/all_to_all | solution.py:146

commit v8 on v6

--- a/solution.py
+++ b/solution.py
@@ -65,7 +65,7 @@
                 out_ref[zu, block, half * 32 : half * 32 + 32, :] = got_ref[block, zu, pl.ds(row, 32), :]
 
 
-def pair_kernel(left_ref, right_ref, map_ref, out_ref, a32, a16, x16, wide_ref, res):
+def prepare_kernel(left_ref, a16, a32):
     for t in range(8):
         zl = t % 2 * 4 + t // 2 % 2 * 2 + t // 4
         for block in range(2):
@@ -75,6 +75,9 @@
                 ].astype(F32)
     for block in range(2):
         a16[:, block * 128 : block * 128 + 128] = a32[block * 512 : block * 512 + 512, :].astype(BF16)
+
+
+def pair_kernel(a16, right_ref, map_ref, out_ref, x16, wide_ref, res):
     wide_ref[...] = jnp.zeros_like(wide_ref)
     for c in range(32):
         for r in range(4):
@@ -162,12 +165,17 @@
         left = lax.all_gather(left, axis, axis=0)
     left = left.reshape(8, 2, 64, 128)
 
+    left = pl.pallas_call(
+        prepare_kernel,
+        out_shape=shape(512, 256),
+        scratch_shapes=[pltpu.VMEM((1024, 128), F32)],
+        compiler_params=params(12),
+        name="prepare",
+    )(left)
     parts = pl.pallas_call(
         pair_kernel,
         out_shape=shape(16, 16, 512),
         scratch_shapes=[
-            pltpu.VMEM((1024, 128), F32),
-            pltpu.VMEM((512, 256), BF16),
             pltpu.VMEM((256, 4096), BF16),
             pltpu.VMEM((4096, 512), BF16),
             pltpu.VMEM((1024, 128), F32),

time: 67.7 us -> 67.7 us (level)
  no operation moved by 1% of the time
where the time goes in v8:
time: 67.7 us; the launch traced here: 67.4 us
  blocking collectives  42.7 us (63%)
  starting transfers between devices  16.4 us (24%)
  Pallas kernels  6.02 us (9%)
  waiting for transfers between devices  2.13 us (3%)
    all_to_all x1, blocking collectives, local(): parts = lax.all_to_all(parts, RING, 0, 0)  28 us
    all_gather x2, blocking collectives, local(): left = lax.all_gather(left, axis, axis=0)  12.8 us
    ppermute x1, starting transfers between devices, local(): other = lax.ppermute(left, 'zu', SWAP)  9.1 us
    all_to_all x1, starting transfers between devices, local(): right = lax.all_to_all(right, ('x', 'core', 'y'), 0, 0)  7.33 us
    pallas_call x1, Pallas kernels, local(): pl.pallas_call(projection_kernel, out_shape=(shape(32, 128, 128), shape(1...  2.77 us
    pallas_call x1, Pallas kernels, local(): pl.pallas_call(pair_kernel, out_shape=shape(16, 16, 512), scratch_shapes=...  2.15 us
    all_to_all x1, waiting for transfers between devices, local(): right = lax.all_to_all(right, ('x', 'core', 'y'), 0, 0)  2.13 us
    all_gather x1, blocking collectives, local(): left = lax.all_gather(left, 'core', axis=0)  1.9 us
  transfers between devices with their start and end apart: 2, of which 1 were waited for; matrix products, arithmetic and copies ran while one was open for 0% of the time, Pallas kernels for 0%

profile of v8, /device:TPU:32, one launch (start us, length us, event | category | flops | bytes accessed | tf_op | source)
XLA Modules:
  0.0 67.4 jit_solution(3219793523960254582)
XLA Ops:
  0.0 2.8 %projections.1 = (bf16[32,128,128]{2,1,0:T(8,128)(2,1)}, bf16[128,128]{1,0:T(8,128)(2,1)S(1)}, bf16[1024,128]{1,0:T(8,128)(2,1)S(1)}, f32[1,128]{1,0:T(1,128)S(1)}) custom-call(bf16[128,4,256]{2,1,0:T(4,128)(2,1)} %x_hbm.1, f32[1,256]{1,0:T(1,128)} %bitcast.16, f32[1,256]{1,0:T(1,128)} %bitcast.17, bf16[32,256]{1,0:T(8,128)(2,1)} %bitcast.14, ...), custom_call_target="tpu_custom_call" | custom-call | tf_op jit(solution)/shard_map/projections/pallas_call | solution.py:140
  2.8 9.1 %collective-permute-start = (bf16[128,128]{1,0:T(8,128)(2,1)S(1)}, bf16[128,128]{1,0:T(8,128)(2,1)S(1)}, u32[]{:S(2)}, u32[]{:S(2)}) collective-permute-start(bf16[128,128]{1,0:T(8,128)(2,1)S(1)} %get-tuple-element.9.own_ref), channel_id=1, source_target_pairs={{0,16},{16,0},{1,17},{17,1},{2,18},{18,2},{3,19},{19,3},{4,20},{20... | collective-permute-start | bytes 98312 | tf_op jit(solution)/shard_map/ppermute | solution.py:149
  11.9 7.3 %all-to-all-start = ((bf16[32,128,128]{2,1,0:T(8,128)(2,1)}), bf16[32,128,128]{2,1,0:T(8,128)(2,1)S(1)}, u32[]{:S(2)}, u32[]{:S(2)}) async-start(bf16[32,128,128]{2,1,0:T(8,128)(2,1)} %get-tuple-element.10), calls=%async_computation | async-start | bytes 2097152 | tf_op jit(solution)/shard_map/all_to_all | solution.py:148
  19.2 0.0 collective-permute-done.other_ref
  19.3 1.9 %all-gather = bf16[4,128,128]{2,1,0:T(8,128)(2,1)S(1)} all-gather(bf16[2,128,128]{2,1,0:T(8,128)(2,1)S(1)} %join.1), channel_id=2, replica_groups=mesh['y'=4,'x'=4,'zu'=2,'zv'=2,'zp'=2,'zh'=2,'core'=2] {'core'}, dimensions={0}, use_global_device_ids=true | all-gather | bytes 196608 | tf_op jit(solution)/shard_map/all_gather | solution.py:157
  21.2 6.7 %all-gather.1 = bf16[4,2,64,128]{3,2,1,0:T(8,128)(2,1)S(1)} all-gather(bf16[2,2,64,128]{3,2,1,0:T(8,128)(2,1)S(1)} %select.1), channel_id=3, replica_groups=mesh['y'=4,'x'=4,'zu'=2,'zv'=2,'zp'=2,'zh'=2,'core'=2] {'zv'}, dimensions={0}, use_global_device_ids=true | all-gather | bytes 196608 | tf_op jit(solution)/shard_map/all_gather | solution.py:165
  27.9 6.1 %all-gather.2 = bf16[4,2,2,64,128]{4,3,2,1,0:T(8,128)(2,1)S(1)} all-gather(bf16[2,2,2,64,128]{4,3,2,1,0:T(8,128)(2,1)S(1)} %bitcast.13), channel_id=4, replica_groups=mesh['y'=4,'x'=4,'zu'=2,'zv'=2,'zp'=2,'zh'=2,'core'=2] {'zp'}, dimensions={0}, use_global_device_ids=true | all-gather | bytes 393216 | tf_op jit(solution)/shard_map/all_gather | solution.py:165
  34.0 0.3 prepare.1.a16
  34.2 2.1 %all-to-all-done.right_ref = bf16[32,128,128]{2,1,0:T(8,128)(2,1)S(1)} async-done(((bf16[32,128,128]{2,1,0:T(8,128)(2,1)}), bf16[32,128,128]{2,1,0:T(8,128)(2,1)S(1)}, u32[]{:S(2)}, u32[]{:S(2)}) %all-to-all-start) | async-done | bytes 1048608 | tf_op jit(solution)/shard_map/all_to_all | solution.py:148
  36.4 2.2 %pair_block.1 = bf16[16,16,512]{2,1,0:T(8,128)(2,1)S(1)} custom-call(bf16[512,256]{1,0:T(8,128)(2,1)S(1)} %prepare.1.a16, bf16[32,128,128]{2,1,0:T(8,128)(2,1)S(1)} %all-to-all-done.right_ref, bf16[1024,128]{1,0:T(8,128)(2,1)S(1)} %get-tuple-element.11.map_ref), custom_call_target="tpu_custom_call" | custom-call | tf_op jit(solution)/shard_map/pair_block/pallas_call | solution.py:175
  38.5 28.0 %all_to_all.10.parts_ref = bf16[16,16,512]{2,1,0:T(8,128)(2,1)S(1)} all-to-all(bf16[16,16,512]{2,1,0:T(8,128)(2,1)S(1)} %pair_block.1), channel_id=1, replica_groups=mesh['y'=4,'x'=4,'zu'=2,'zv'=2,'zp'=2,'zh'=2,'core'=2] {'zp','zh','zv','..., dimensions={0} | all-to-all | bytes 524288 | tf_op jit(solution)/shard_map/all_to_all | solution.py:186
  66.5 0.8 %sum_and_bias.1 = bf16[512,128]{1,0:T(8,128)(2,1)} custom-call(bf16[16,16,512]{2,1,0:T(8,128)(2,1)S(1)} %all_to_all.10.parts_ref, f32[1,128]{1,0:T(1,128)S(1)} %get-tuple-element.12.bias_ref), custom_call_target="tpu_custom_call" | custom-call | tf_op jit(solution)/shard_map/sum_and_bias/pallas_call | solution.py:187
  (2 shorter events, 0.0 us)
Async XLA Ops:
  2.8 16.4 %collective-permute-start = (bf16[128,128]{1,0:T(8,128)(2,1)S(1)}, bf16[128,128]{1,0:T(8,128)(2,1)S(1)}, u32[]{:S(2)}, u32[]{:S(2)}) collective-permute-start(bf16[128,128]{1,0:T(8,128)(2,1)S(1)} %get-tuple-element.9.own_ref), channel_id=1, source_target_pairs={{0,16},{16,0},{1,17},{17,1},{2,18},{18,2},{3,19},{19,3},{4,20},{20... | collective-permute-start | bytes 98312 | tf_op jit(solution)/shard_map/ppermute | solution.py:149
  11.9 24.5 %all-to-all-start = ((bf16[32,128,128]{2,1,0:T(8,128)(2,1)}), bf16[32,128,128]{2,1,0:T(8,128)(2,1)S(1)}, u32[]{:S(2)}, u32[]{:S(2)}) async-start(bf16[32,128,128]{2,1,0:T(8,128)(2,1)} %get-tuple-element.10), calls=%async_computation | async-start | bytes 2097152 | tf_op jit(solution)/shard_map/all_to_all | solution.py:148

commit v9 on v8

--- a/solution.py
+++ b/solution.py
@@ -94,15 +94,15 @@
                 x16[yx * 16 : yx * 16 + 16, c * 128 : c * 128 + 128] = outer[
                     c * 16 : c * 16 + 16, k * 128 : k * 128 + 128
                 ]
-    total = jnp.dot(x16[...], wide_ref[...], preferred_element_type=F32) * (1.0 / 512)
-    for r in range(4):
-        res[r * 256 : r * 256 + 256, :] = total[:, r * 128 : r * 128 + 128]
-    for k in range(8):
-        for half in range(2):
-            to = ring_rank(k, half)
-            for r in range(4):
-                rows = res[pl.ds(r * 256 + k * 2 + half, 16, stride=16), :]
-                out_ref[to, :, r * 128 : r * 128 + 128] = rows.astype(BF16)
+    for first in range(0, 4, 2):
+        lanes = wide_ref[:, first * 128 : first * 128 + 256]
+        total = jnp.dot(x16[...], lanes, preferred_element_type=F32) * (1.0 / 512)
+        for r in range(first, first + 2):
+            res[r * 256 : r * 256 + 256, :] = total[:, (r - first) * 128 : (r - first) * 128 + 128]
+            for k in range(8):
+                for half in range(2):
+                    rows = res[pl.ds(r * 256 + k * 2 + half, 16, stride=16), :]
+                    out_ref[ring_rank(k, half), :, r * 128 : r * 128 + 128] = rows.astype(BF16)
 
 
 def ring_rank(zl, half):

time: 67.7 us -> 67.7 us (level)
  no operation moved by 1% of the time
where the time goes in v9:
time: 67.7 us; the launch traced here: 67.4 us
  blocking collectives  42.7 us (63%)
  starting transfers between devices  16.4 us (24%)
  Pallas kernels  6.02 us (9%)
  waiting for transfers between devices  2.13 us (3%)
    all_to_all x1, blocking collectives, local(): parts = lax.all_to_all(parts, RING, 0, 0)  28 us
    all_gather x2, blocking collectives, local(): left = lax.all_gather(left, axis, axis=0)  12.8 us
    ppermute x1, starting transfers between devices, local(): other = lax.ppermute(left, 'zu', SWAP)  9.1 us
    all_to_all x1, starting transfers between devices, local(): right = lax.all_to_all(right, ('x', 'core', 'y'), 0, 0)  7.33 us
    pallas_call x1, Pallas kernels, local(): pl.pallas_call(projection_kernel, out_shape=(shape(32, 128, 128), shape(1...  2.77 us
    pallas_call x1, Pallas kernels, local(): pl.pallas_call(pair_kernel, out_shape=shape(16, 16, 512), scratch_shapes=...  2.15 us
    all_to_all x1, waiting for transfers between devices, local(): right = lax.all_to_all(right, ('x', 'core', 'y'), 0, 0)  2.13 us
    all_gather x1, blocking collectives, local(): left = lax.all_gather(left, 'core', axis=0)  1.9 us
  transfers between devices with their start and end apart: 2, of which 1 were waited for; matrix products, arithmetic and copies ran while one was open for 0% of the time, Pallas kernels for 0%

profile of v9, /device:TPU:32, one launch (start us, length us, event | category | flops | bytes accessed | tf_op | source)
XLA Modules:
  0.0 67.4 jit_solution(3219793523960254582)
XLA Ops:
  0.0 2.8 %projections.1 = (bf16[32,128,128]{2,1,0:T(8,128)(2,1)}, bf16[128,128]{1,0:T(8,128)(2,1)S(1)}, bf16[1024,128]{1,0:T(8,128)(2,1)S(1)}, f32[1,128]{1,0:T(1,128)S(1)}) custom-call(bf16[128,4,256]{2,1,0:T(4,128)(2,1)} %x_hbm.1, f32[1,256]{1,0:T(1,128)} %bitcast.16, f32[1,256]{1,0:T(1,128)} %bitcast.17, bf16[32,256]{1,0:T(8,128)(2,1)} %bitcast.14, ...), custom_call_target="tpu_custom_call" | custom-call | tf_op jit(solution)/shard_map/projections/pallas_call | solution.py:140
  2.8 9.1 %collective-permute-start = (bf16[128,128]{1,0:T(8,128)(2,1)S(1)}, bf16[128,128]{1,0:T(8,128)(2,1)S(1)}, u32[]{:S(2)}, u32[]{:S(2)}) collective-permute-start(bf16[128,128]{1,0:T(8,128)(2,1)S(1)} %get-tuple-element.9.own_ref), channel_id=1, source_target_pairs={{0,16},{16,0},{1,17},{17,1},{2,18},{18,2},{3,19},{19,3},{4,20},{20... | collective-permute-start | bytes 98312 | tf_op jit(solution)/shard_map/ppermute | solution.py:149
  11.9 7.3 %all-to-all-start = ((bf16[32,128,128]{2,1,0:T(8,128)(2,1)}), bf16[32,128,128]{2,1,0:T(8,128)(2,1)S(1)}, u32[]{:S(2)}, u32[]{:S(2)}) async-start(bf16[32,128,128]{2,1,0:T(8,128)(2,1)} %get-tuple-element.10), calls=%async_computation | async-start | bytes 2097152 | tf_op jit(solution)/shard_map/all_to_all | solution.py:148
  19.2 0.0 collective-permute-done.other_ref
  19.3 1.9 %all-gather = bf16[4,128,128]{2,1,0:T(8,128)(2,1)S(1)} all-gather(bf16[2,128,128]{2,1,0:T(8,128)(2,1)S(1)} %join.1), channel_id=2, replica_groups=mesh['y'=4,'x'=4,'zu'=2,'zv'=2,'zp'=2,'zh'=2,'core'=2] {'core'}, dimensions={0}, use_global_device_ids=true | all-gather | bytes 196608 | tf_op jit(solution)/shard_map/all_gather | solution.py:157
  21.2 6.7 %all-gather.1 = bf16[4,2,64,128]{3,2,1,0:T(8,128)(2,1)S(1)} all-gather(bf16[2,2,64,128]{3,2,1,0:T(8,128)(2,1)S(1)} %select.1), channel_id=3, replica_groups=mesh['y'=4,'x'=4,'zu'=2,'zv'=2,'zp'=2,'zh'=2,'core'=2] {'zv'}, dimensions={0}, use_global_device_ids=true | all-gather | bytes 196608 | tf_op jit(solution)/shard_map/all_gather | solution.py:165
  27.9 6.1 %all-gather.2 = bf16[4,2,2,64,128]{4,3,2,1,0:T(8,128)(2,1)S(1)} all-gather(bf16[2,2,2,64,128]{4,3,2,1,0:T(8,128)(2,1)S(1)} %bitcast.13), channel_id=4, replica_groups=mesh['y'=4,'x'=4,'zu'=2,'zv'=2,'zp'=2,'zh'=2,'core'=2] {'zp'}, dimensions={0}, use_global_device_ids=true | all-gather | bytes 393216 | tf_op jit(solution)/shard_map/all_gather | solution.py:165
  34.0 0.3 prepare.1.a16
  34.2 2.1 %all-to-all-done.right_ref = bf16[32,128,128]{2,1,0:T(8,128)(2,1)S(1)} async-done(((bf16[32,128,128]{2,1,0:T(8,128)(2,1)}), bf16[32,128,128]{2,1,0:T(8,128)(2,1)S(1)}, u32[]{:S(2)}, u32[]{:S(2)}) %all-to-all-start) | async-done | bytes 1048608 | tf_op jit(solution)/shard_map/all_to_all | solution.py:148
  36.4 2.2 %pair_block.1 = bf16[16,16,512]{2,1,0:T(8,128)(2,1)S(1)} custom-call(bf16[512,256]{1,0:T(8,128)(2,1)S(1)} %prepare.1.a16, bf16[32,128,128]{2,1,0:T(8,128)(2,1)S(1)} %all-to-all-done.right_ref, bf16[1024,128]{1,0:T(8,128)(2,1)S(1)} %get-tuple-element.11.map_ref), custom_call_target="tpu_custom_call" | custom-call | tf_op jit(solution)/shard_map/pair_block/pallas_call | solution.py:175
  38.5 28.0 %all_to_all.10.parts_ref = bf16[16,16,512]{2,1,0:T(8,128)(2,1)S(1)} all-to-all(bf16[16,16,512]{2,1,0:T(8,128)(2,1)S(1)} %pair_block.1), channel_id=1, replica_groups=mesh['y'=4,'x'=4,'zu'=2,'zv'=2,'zp'=2,'zh'=2,'core'=2] {'zp','zh','zv','..., dimensions={0} | all-to-all | bytes 524288 | tf_op jit(solution)/shard_map/all_to_all | solution.py:186
  66.5 0.8 %sum_and_bias.1 = bf16[512,128]{1,0:T(8,128)(2,1)} custom-call(bf16[16,16,512]{2,1,0:T(8,128)(2,1)S(1)} %all_to_all.10.parts_ref, f32[1,128]{1,0:T(1,128)S(1)} %get-tuple-element.12.bias_ref), custom_call_target="tpu_custom_call" | custom-call | tf_op jit(solution)/shard_map/sum_and_bias/pallas_call | solution.py:187
  (2 shorter events, 0.0 us)
Async XLA Ops:
  2.8 16.4 %collective-permute-start = (bf16[128,128]{1,0:T(8,128)(2,1)S(1)}, bf16[128,128]{1,0:T(8,128)(2,1)S(1)}, u32[]{:S(2)}, u32[]{:S(2)}) collective-permute-start(bf16[128,128]{1,0:T(8,128)(2,1)S(1)} %get-tuple-element.9.own_ref), channel_id=1, source_target_pairs={{0,16},{16,0},{1,17},{17,1},{2,18},{18,2},{3,19},{19,3},{4,20},{20... | collective-permute-start | bytes 98312 | tf_op jit(solution)/shard_map/ppermute | solution.py:149
  11.9 24.5 %all-to-all-start = ((bf16[32,128,128]{2,1,0:T(8,128)(2,1)}), bf16[32,128,128]{2,1,0:T(8,128)(2,1)S(1)}, u32[]{:S(2)}, u32[]{:S(2)}) async-start(bf16[32,128,128]{2,1,0:T(8,128)(2,1)} %get-tuple-element.10), calls=%async_computation | async-start | bytes 2097152 | tf_op jit(solution)/shard_map/all_to_all | solution.py:148
